TPU v7x, 32 devices: a whole 2x2x4 slice. The times are simulated.
32 devices in a mesh: dp: 8 (over z, x), group: 4 (over y, core).
Axes of the slice: x: 2, y: 2, z: 4, core: 2. Of those that a mesh axis runs over, the one named last changes fastest.
Arguments:
- tokens: bfloat16 [8, 1024, 1536], P('dp', 'group'), may hold values from -6 to 6
- cotangent: bfloat16 [8, 1024, 1536], P('dp', 'group'), may hold values from -6 to 6
- lengths: int32 [8], P('dp'), may hold values from 256 to 1024, as said below
- intake_weight: float32 [7077888], P(('dp', 'group')), may hold values from -0.15625 to 0.15625
- intake_first: float32 [7077888], P(('dp', 'group')), may hold values from -320 to 320
- intake_second: float32 [7077888], P(('dp', 'group')), may hold values from 2508.8 to 10035.2
- output_weight: float32 [2359296], P(('dp', 'group')), may hold values from -0.15625 to 0.15625
- output_first: float32 [2359296], P(('dp', 'group')), may hold values from -320 to 320
- output_second: float32 [2359296], P(('dp', 'group')), may hold values from 2508.8 to 10035.2
- swiglu_weight: float32 [21233664], P(('dp', 'group')), may hold values from -0.15625 to 0.15625
- swiglu_first: float32 [21233664], P(('dp', 'group')), may hold values from -320 to 320
- swiglu_second: float32 [21233664], P(('dp', 'group')), may hold values from 2508.8 to 10035.2
- down_weight: float32 [10616832], P(('dp', 'group')), may hold values from -0.078125 to 0.078125
- down_first: float32 [10616832], P(('dp', 'group')), may hold values from -320 to 320
- down_second: float32 [10616832], P(('dp', 'group')), may hold values from 2508.8 to 10035.2
- norm_gains: float32 [3072], P(('dp', 'group')), may hold values from 0.5 to 1.5
- gains_first: float32 [3072], P(('dp', 'group')), may hold values from -448 to 448
- gains_second: float32 [3072], P(('dp', 'group')), may hold values from 5120 to 20480
- conv_kernel: float32 [4608], P(('dp', 'group')), may hold values from -3.5 to 3.5
- kernel_first: float32 [4608], P(('dp', 'group')), may hold values from -448 to 448
- kernel_second: float32 [4608], P(('dp', 'group')), may hold values from 5120 to 20480
Outputs:
- block_out: bfloat16 [8, 1024, 1536], P('dp', 'group')
- input_grad: bfloat16 [8, 1024, 1536], P('dp', 'group')
- intake_first_new: float32 [7077888], P(('dp', 'group'))
- intake_second_new: float32 [7077888], P(('dp', 'group'))
- intake_weight_new: float32 [7077888], P(('dp', 'group'))
- output_first_new: float32 [2359296], P(('dp', 'group'))
- output_second_new: float32 [2359296], P(('dp', 'group'))
- output_weight_new: float32 [2359296], P(('dp', 'group'))
- swiglu_first_new: float32 [21233664], P(('dp', 'group'))
- swiglu_second_new: float32 [21233664], P(('dp', 'group'))
- swiglu_weight_new: float32 [21233664], P(('dp', 'group'))
- down_first_new: float32 [10616832], P(('dp', 'group'))
- down_second_new: float32 [10616832], P(('dp', 'group'))
- down_weight_new: float32 [10616832], P(('dp', 'group'))
- gains_first_new: float32 [3072], P(('dp', 'group'))
- gains_second_new: float32 [3072], P(('dp', 'group'))
- norm_gains_new: float32 [3072], P(('dp', 'group'))
- kernel_first_new: float32 [4608], P(('dp', 'group'))
- kernel_second_new: float32 [4608], P(('dp', 'group'))
- conv_kernel_new: float32 [4608], P(('dp', 'group'))
Inputs may be any that keep to these rules, and one draw needn't show every extreme that they name: `lengths`: each row's valid positions are a prefix of its 1024 slots; some row is full and some row holds exactly 256.
All inputs are finite; a program needn't handle non-finite values.
Results may differ from a plain program's by a relative error of at most 0.018.
Values may be sent and summed in bfloat16 or wider, within the bound.
A program may use at most 256 MiB of HBM per device.

v0:
```python
import functools

import jax
import jax.numpy as jnp
from jax import lax
from jax.experimental import pallas as pl
from jax.experimental.pallas import tpu as pltpu
from jax.sharding import PartitionSpec as P

D = 1536
FF = 6912
STEP = 5
WIDTH = 256
ROW_TILE = 16

EPS_NORM = 1e-05
BETA_ONE = 0.5
BETA_TWO = 0.5
ADAM_EPS = 1e-08
RATE_MATRIX = 0.02
RATE_VECTOR = 0.2
DECAY = 0.1

MESH = pl.DeviceIdType.MESH
BF = jnp.bfloat16
F32 = jnp.float32


def update(weight, first, second, grad, rate, decay):
    first_new = BETA_ONE * first + (1.0 - BETA_ONE) * grad
    second_new = BETA_TWO * second + (1.0 - BETA_TWO) * grad * grad
    first_hat = first_new / (1.0 - BETA_ONE**STEP)
    second_hat = second_new / (1.0 - BETA_TWO**STEP)
    weight_new = weight - rate * (first_hat / (jnp.sqrt(second_hat) + ADAM_EPS) + decay * weight)
    return (first_new, second_new, weight_new)


def dot(left, right):
    return lax.dot_general(left, right, (((1,), (0,)), ((), ())), preferred_element_type=F32)


def dot_t(left, right):
    return lax.dot_general(left, right, (((1,), (1,)), ((), ())), preferred_element_type=F32)


def await_bytes(ref, sem):
    pltpu.make_async_copy(ref, ref, sem).wait()


def block_kernel(
    sizes,
    tok, bck_own, wi_own, wo_own, ff_own, small_own,
    block_out, input_grad, g_ff, g_wi, g_wo, g_small,
    wf_all, wi_all, wo_all, tok_all, nrm_far, bck_all, n2_all, dbr_all,
    rs_br, rs_y, rs_n2, rs_n1, via,
    sib_f, sib_i, sib_o, up_f, up_i, down_f, down_i, far_f, far_i, z_o, mixed_far,
    ws, wi, wo, act, act_t, bck, bck_t, acc_y, acc_n, grad, sibv, part, stage,
    prod, gated, dmix, mid, dmid, low, sibo, parto,
    small_all, gains, taps, g_gains, g_taps, sm_mine, sm_plane, sm_sum, sm_z,
    extra, ag_ssem, ag_rsem, ag_fsem, rs_ssem, rs_rsem, via_ssem, via_rsem, z_ssem, z_rsem, f_ssem, f_rsem,
    gs_ssem, gs_rsem, gz_ssem, up_sem, down_sem, own_ssem, own_rsem, back_ssem, back_rsem, osem,
    sa_ssem, sa_rsem, sz_ssem, sz_rsem, ta_ssem, ta_rsem, tz_ssem, tz_rsem, wsem, lsem,
):
    (out_n, group, rows_n, seg, ch, cblk, chunks) = sizes
    block = rows_n // group
    direct = block % 16 == 0
    count = 2 * out_n * group
    blocks = ch // 128
    seq = group * seg
    dp = lax.axis_index("dp")
    g = lax.axis_index("group")
    o, a = dp // 2, lax.rem(dp, 2)
    y, b = g // 2, lax.rem(g, 2)
    t = 2 * y + a
    mate = (dp, g + 1 - 2 * b)

    def peer(k):
        o2 = lax.rem(o + k, out_n)
        return o2, (2 * o2 + a, g)

    barrier = pltpu.get_barrier_semaphore()
    for x2 in range(2):
        for g2 in range(group):
            @pl.when((x2 != a) | (g2 != g))
            def _():
                pl.semaphore_signal(barrier, inc=1, device_id=(2 * o + x2, g2), device_id_type=MESH)

    def greet(k, carry):
        pl.semaphore_signal(barrier, inc=1, device_id=peer(k)[1], device_id_type=MESH)
        return carry

    lax.fori_loop(1, out_n, greet, 0)
    pl.semaphore_wait(barrier, 2 * group - 1 + out_n - 1)

    def remote(src, dst, ssem, rsem, dev):
        return pltpu.make_async_remote_copy(
            src_ref=src, dst_ref=dst, send_sem=ssem, recv_sem=rsem, device_id=dev, device_id_type=MESH
        )

    def switch(alone, local, copy, op):
        if op == "start":
            @pl.when(alone)
            def _():
                local.start()

            @pl.when(jnp.logical_not(alone))
            def _():
                copy.start()
        else:
            @pl.when(jnp.logical_not(alone))
            def _():
                copy.wait_send()

    odd = lax.rem(a + b, 2)
    size = seg // 2
    y_via = odd * y + (1 - odd) * (1 - y)
    h_via = 1 - odd
    partner = (2 * o + odd * a + (1 - odd) * (1 - a), 2 * (odd * (1 - y) + (1 - odd) * y) + b)

    def part_of(h):
        return pl.ds(h * size, size) if isinstance(h, int) else pl.ds(pl.multiple_of(h * size, size), size)

    def spread(src, dst, n, op):
        for d, h in ((1, 0), (2, 1), (1, 1), (2, 0), (0, 0), (0, 1)):
            x2, y2 = (1 - a if d == 1 else a), (1 - y if d == 2 else y)
            one, two = src.at[part_of(h)], dst.at[g, part_of(h)]
            copy = remote(one, two, ag_ssem.at[n, d, h], ag_rsem.at[n, g, h], (2 * o + x2, 2 * y2 + a))
            if d == 0:
                switch(a == b, pltpu.make_async_copy(one, two, ag_rsem.at[n, g, h]), copy, op)
            elif op == "start":
                copy.start()
            else:
                copy.wait_send()
        if op == "end":
            for k in range(2):
                ref = dst.at[2 * y_via + k, part_of(h_via)]
                await_bytes(ref, ag_fsem.at[n, k])

    def spread_on(dst, n):
        for k in range(2):
            q = 2 * y_via + k
            ref = dst.at[q, part_of(h_via)]
            await_bytes(ref, ag_rsem.at[n, q, h_via])
            remote(ref, ref, ag_fsem.at[n, k], ag_rsem.at[n, q, h_via], partner).start()

    def spread_wait(dst, n, q):
        for h in range(2):
            @pl.when((q // 2 != y_via) | (h != h_via))
            def _():
                await_bytes(dst.at[q, part_of(h)], ag_rsem.at[n, q, h])

    def give(terms, dst, n, at, q, h, slot, op="start"):
        one, two = terms(q).at[part_of(h)], dst.at[slot, part_of(h)]
        copy = remote(one, two, rs_ssem.at[n, at, h], rs_rsem.at[n, slot, h], (2 * o + b, q))
        if slot == 0:
            switch(q == g, pltpu.make_async_copy(one, two, rs_rsem.at[n, 0, h]), copy, op)
        elif op == "start":
            copy.start()
        else:
            copy.wait_send()

    def give_half(terms, n, k, h, op):
        q = 2 * (1 - y) + k
        dev = (2 * o + 1 - a, g) if h == 0 else (dp, 2 * (1 - y) + b)
        copy = remote(terms(q).at[part_of(h)], via.at[n, k], via_ssem.at[n, k, h], via_rsem.at[n, k], dev)
        if op == "start":
            copy.start()
        else:
            copy.wait_send()

    def scatter(terms, dst, n, produce):
        for k in range(2):
            q = 2 * (1 - y) + k
            produce(q)

            @pl.when(odd == 1)
            def _():
                give_half(terms, n, k, 0, "start")
                give_half(terms, n, k, 1, "start")

            @pl.when(odd == 0)
            def _():
                give(terms, dst, n, k, q, 1, 1)

        for k in range(2):
            q = 2 * y + k
            produce(q)

            @pl.when(odd == 1)
            def _():
                give(terms, dst, n, 2 + k, q, 0, 2)

            @pl.when(odd == 0)
            def _():
                give(terms, dst, n, 2 + k, q, 0, 0)
                give(terms, dst, n, 2 + k, q, 1, 0)

    def scatter_on(terms, dst, n):
        for k in range(2):
            q = 2 * y_via + k
            await_bytes(via.at[n, k], via_rsem.at[n, k])
            fetch(via.at[n, k], extra, 0)

            def add_rows(i, carry):
                here = pl.ds(pl.multiple_of(odd * size + i * ROW_TILE, ROW_TILE), ROW_TILE)
                ref = terms(q)
                ref[here, :] = (ref[here, :].astype(F32) + extra[rows16(i), :].astype(F32)).astype(BF)
                return carry

            lax.fori_loop(0, size // ROW_TILE, add_rows, 0)

            @pl.when(odd == 1)
            def _():
                give(terms, dst, n, 2 + k, q, 1, 2)

            @pl.when(odd == 0)
            def _():
                give(terms, dst, n, k, q, 0, 1)

    def scatter_end(terms, dst, n):
        @pl.when(odd == 1)
        def _():
            for k in range(2):
                for h in range(2):
                    give_half(terms, n, k, h, "end")
                    give(terms, dst, n, 2 + k, 2 * y + k, h, 2, "end")

        @pl.when(odd == 0)
        def _():
            for k in range(2):
                for h in range(2):
                    give(terms, dst, n, k, 2 * (1 - y) + k, h, 1, "end")
                    give(terms, dst, n, 2 + k, 2 * y + k, h, 0, "end")

    def scatter_wait(dst, n):
        for slot in range(3):
            for h in range(2):
                await_bytes(dst.at[slot, part_of(h)], rs_rsem.at[n, slot, h])

    def staged(q):
        return stage.at[q]

    def any_span(q):
        return pl.ds(pl.multiple_of(q * seg, seg), seg)

    def slot_of(i, o2, p):
        if isinstance(i, int) and i == 0:
            return wi_all.at[o2, p]
        if isinstance(i, int) and i == 1:
            return wo_all.at[o2, p]
        return wf_all.at[i - 2, :, o2, p]

    def half_of(i, p):
        if isinstance(i, int) and i == 0:
            return wi_all.at[:, p]
        if isinstance(i, int) and i == 1:
            return wo_all.at[:, p]
        return wf_all.at[i - 2, :, :, p]

    my_rows = pl.ds(pl.multiple_of(g * block, 4), block)

    def own_send(i, op):
        if isinstance(i, int) and i == 1:
            dst = wo_all.at[o, a]
            switch(
                a == b,
                pltpu.make_async_copy(wo_own, dst, own_rsem.at[1, 0]),
                remote(wo_own, dst, own_ssem.at[1, 0], own_rsem.at[1, 0], (2 * o + b, 2 * y + a)),
                op,
            )
            return
        if not direct:
            src = wi_own if isinstance(i, int) and i == 0 else ff_own.at[i - 2]
            if op == "start":
                pltpu.make_async_copy(src, slot_of(i, o, b), own_rsem.at[i, 0]).start()
            return
        for t2 in range(group):
            ty, tx = t2 // 2, t2 % 2
            if isinstance(i, int) and i == 0:
                src, dst = wi_own.at[t2], wi_all.at[o, a, my_rows]
            else:
                src, dst = ff_own.at[t2, i - 2], wf_all.at[i - 2, :, o, a, my_rows]
            switch(
                (tx == a) & (ty == y) & (a == b),
                pltpu.make_async_copy(src, dst, own_rsem.at[i, g]),
                remote(src, dst, own_ssem.at[i, t2], own_rsem.at[i, g], (2 * o + tx, 2 * ty + a)),
                op,
            )

    def own_wait(i):
        if not direct or isinstance(i, int) and i == 1:
            await_bytes(slot_of(i, o, b), own_rsem.at[i, 0])
            return
        for q in range(group):
            if isinstance(i, int) and i == 0:
                await_bytes(wi_all.at[o, b, pl.ds(q * block, block)], own_rsem.at[i, q])
            else:
                await_bytes(wf_all.at[i - 2, :, o, b, pl.ds(q * block, block)], own_rsem.at[i, q])

    first, final = o == 0, o == out_n - 1

    def piece_send(i, src, side):
        ref = slot_of(i, src, b)
        dev = (2 * (o + 1 - 2 * side) + a, g)
        remote(ref, ref, z_ssem.at[i, side, src], z_rsem.at[i, src], dev).start()

    def when(condition, call, *args):
        @pl.when(condition)
        def _():
            call(*args)

    def hop(i, h):
        if h == 0:
            own_wait(i)
            when(jnp.logical_not(final), piece_send, i, o, 0)
            when(jnp.logical_not(first), piece_send, i, o, 1)
            return

        @pl.when(o - h >= 0)
        def _():
            await_bytes(slot_of(i, o - h, b), z_rsem.at[i, o - h])
            when(jnp.logical_not(final), piece_send, i, o - h, 0)

        @pl.when(o + h < out_n)
        def _():
            await_bytes(slot_of(i, o + h, b), z_rsem.at[i, o + h])
            when(jnp.logical_not(first), piece_send, i, o + h, 1)

        if h == out_n - 1:
            remote(half_of(i, b), half_of(i, b), f_ssem.at[i], f_rsem.at[i], mate).start()

    items = 2 + chunks
    sent = set()

    def own_start(*which):
        for i in which:
            if i < items and i not in sent:
                sent.add(i)
                own_send(i, "start")

    def pump(time):
        if isinstance(time, int):
            own_start(*range(time + 1))
        for h in range(out_n - 1, -1, -1):
            if isinstance(time, int):
                if 0 <= time - h < items:
                    hop(time - h, h)
            else:
                when(time - h < items, hop, time - h, h)

    def gather_wait(i):
        await_bytes(half_of(i, 1 - b), f_rsem.at[i])

    def gather_close(i):
        def sent(src, side):
            await_bytes(slot_of(i, src, b), z_ssem.at[i, side, src])

        @pl.when(jnp.logical_not(final))
        def _():
            lax.fori_loop(0, o + 1, lambda src, carry: (sent(src, 0), carry)[1], 0)

        @pl.when(jnp.logical_not(first))
        def _():
            lax.fori_loop(o, out_n, lambda src, carry: (sent(src, 1), carry)[1], 0)

        await_bytes(half_of(i, b), f_ssem.at[i])
        own_send(i, "end")

    def fetch(src, dst, n):
        copy = pltpu.make_async_copy(src, dst, lsem.at[n])
        copy.start()
        copy.wait()

    def span(q):
        return pl.ds(q * seg, seg)

    def rows16(i):
        return pl.ds(pl.multiple_of(i * ROW_TILE, ROW_TILE), ROW_TILE)

    def lanes(k, j):
        return pl.ds(k * 384 + j * 128, 128)

    place = a * group + g
    mine = o * (2 * group) + place

    def plane(src, dst, ssem, rsem, op):
        for x2 in range(2):
            for g2 in range(group):
                @pl.when((x2 != a) | (g2 != g))
                def _():
                    copy = remote(src, dst, ssem.at[x2 * group + g2], rsem.at[place], (2 * o + x2, g2))
                    if op == "start":
                        copy.start()
                    else:
                        copy.wait_send()

    def plane_wait(ref, rsem):
        for x2 in range(2):
            for g2 in range(group):
                @pl.when((x2 != a) | (g2 != g))
                def _():
                    await_bytes(ref, rsem.at[x2 * group + g2])

    def far(src, dst, ssem, rsem, op):
        def one(k, carry):
            copy = remote(src, dst, ssem.at[k], rsem.at[o], peer(k)[1])
            if op == "start":
                copy.start()
            else:
                copy.wait_send()
            return carry

        lax.fori_loop(1, out_n, one, 0)

    def far_wait(ref, rsem):
        def one(k, carry):
            await_bytes(ref, rsem.at[peer(k)[0]])
            return carry

        lax.fori_loop(1, out_n, one, 0)

    planes = small_all.at[pl.ds(o * 2 * group, 2 * group)]
    pltpu.make_async_copy(small_own, small_all.at[mine], lsem.at[2]).start()
    plane(small_own, small_all.at[mine], sa_ssem, sa_rsem, "start")

    def convolved(q, col):
        return (
            taps[0:1, col] * prod[pl.ds(q * seg + 6, seg), col]
            + taps[1:2, col] * prod[pl.ds(q * seg + 7, seg), col]
            + taps[2:3, col] * prod[pl.ds(q * seg + 8, seg), col]
        )

    own_start(0)
    own_start(1)
    own_start(2)
    spread(tok, tok_all, 0, "start")
    own_start(3)
    prod[pl.ds(0, 8), :] = jnp.zeros((8, ch), F32)
    pump(0)
    await_bytes(small_own, lsem.at[2])
    plane_wait(small_own, sa_rsem)
    far(planes, planes, sz_ssem, sz_rsem, "start")
    pump(1)
    far_wait(planes, sz_rsem)
    spread_on(tok_all, 0)

    share = 2 * D // count
    rows_of = {}
    for n in range(count):
        row = n * share // 128
        rows_of.setdefault(row, []).append((n, 0))
        if (n * share + share - 1) // 128 > row:
            rows_of.setdefault(row + 1, []).append((n, 1))
    for tile, pieces in rows_of.items():
        value = sum(small_all[n, r : r + 1, :] for n, r in pieces)
        i, j = tile // (D // 128), tile % (D // 128)
        gains[i : i + 1, j * 128 : (j + 1) * 128] = value
    rows_of = {}
    for m in range(3 * count):
        n, piece = m // 3, m % 3
        tap, rest = m // count, m % count
        lane = rest // group * cblk
        rows_of.setdefault((tap, lane // 128), []).append((n, 2 + 2 * piece, rest % group))
        if (lane + block - 1) // 128 > lane // 128:
            rows_of.setdefault((tap, lane // 128 + 1), []).append((n, 3 + 2 * piece, rest % group))
    for (tap, tile), pieces in rows_of.items():
        value = jnp.zeros((1, 128), F32)
        for t2 in range(group):
            value = value + jnp.where(t == t2, sum(small_all[n, r : r + 1, :] for n, r, p in pieces if p == t2), 0.0)
        taps[tap : tap + 1, tile * 128 : (tile + 1) * 128] = value

    pump(2)
    for q in range(group):
        spread_wait(tok_all, 0, q)
        fetch(tok_all.at[q], act.at[span(q)], 0)

        def normed_rows(i, carry, q=q):
            here = pl.ds(pl.multiple_of(q * seg + i * ROW_TILE, ROW_TILE), ROW_TILE)
            row = act[here, :].astype(F32)
            s1 = lax.rsqrt(jnp.mean(row * row, axis=-1, keepdims=True) + EPS_NORM)
            act[here, :] = (row * s1 * gains[0:1, :]).astype(BF)
            return carry

        lax.fori_loop(0, seg // ROW_TILE, normed_rows, 0, unroll=2)
    own_start(4)
    spread(bck_own, bck_all, 1, "start")
    own_start(5)
    keep_normed = pltpu.make_async_copy(act, nrm_far, lsem.at[2])
    keep_normed.start()
    for time in range(3, out_n):
        pump(time)
    gather_wait(0)
    fetch(wi_all, wi, 0)
    keep_normed.wait()

    for q in range(group):
        for k in range(blocks):
            acc_y[span(q), pl.ds(k * 384, 384)] = dot(
                act[span(q), :], wi[:, :, :, pl.ds(k * 384, 384)].reshape(D, 384)
            )
        for k in range(blocks):
            col = pl.ds(k * 128, 128)
            prod[pl.ds(q * seg + 8, seg), col] = acc_y[span(q), lanes(k, 0)] * acc_y[span(q), lanes(k, 2)]
            gated[span(q), col] = (acc_y[span(q), lanes(k, 1)] * convolved(q, col)).astype(BF)
    spread_on(bck_all, 1)
    pump(out_n)
    gather_wait(1)
    fetch(wo_all, wo, 0)

    def branch(q):
        for n in range(4):
            col = pl.ds(n * 384, 384)
            stage[q, :, col] = dot(gated[any_span(q), :], wo[:, :, :, col].reshape(ch, 384)).astype(BF)

    scatter(staged, rs_br, 0, branch)
    scatter_on(staged, rs_br, 0)
    spill = pltpu.make_async_copy(acc_y.at[:, pl.ds(0, 3 * ch)], mixed_far, lsem.at[2])
    spill.start()
    own_start(6)
    pump(out_n + 1)
    for q in range(group):
        spread_wait(bck_all, 1, q)
        fetch(bck_all.at[q], bck.at[span(q)], 0)
        bck_t[:, span(q)] = bck[span(q), :].T

    pump(out_n + 2)
    scatter_wait(rs_br, 0)
    scatter_end(staged, rs_br, 0)
    fetch(rs_br, stage.at[pl.ds(0, 3)], 0)

    def arrived(here):
        total = stage[0, here, :].astype(F32)
        for q in range(1, 3):
            total = total + stage[q, here, :].astype(F32)
        return total

    def middle_rows(i, carry):
        here = rows16(i)
        mi = tok[here, :].astype(F32) + arrived(here)
        mid[here, :] = mi
        s2 = lax.rsqrt(jnp.mean(mi * mi, axis=-1, keepdims=True) + EPS_NORM)
        low[here, :] = (mi * s2 * gains[1:2, :]).astype(BF)
        return carry

    lax.fori_loop(0, seg // ROW_TILE, middle_rows, 0)
    spread(low, n2_all, 2, "start")
    own_start(*range(items))
    pump(out_n + 3)
    spread_on(n2_all, 2)
    pump(out_n + 4)
    gather_wait(2)
    pltpu.make_async_copy(wf_all.at[0], ws.at[0], wsem.at[0]).start()
    spill.wait()

    def clear(i, carry):
        here = rows16(i)
        acc_y[here, :] = jnp.zeros((ROW_TILE, D), F32)
        acc_n[here, :] = jnp.zeros((ROW_TILE, D), F32)
        return carry

    lax.fori_loop(0, seq // ROW_TILE, clear, 0)
    for q in range(group):
        spread_wait(n2_all, 2, q)
        fetch(n2_all.at[q], act.at[span(q)], 0)
        act_t[:, span(q)] = act[span(q), :].T

    def chunk_refs(kind, c):
        if kind == "f":
            return lax.rem(c, 2), c, sib_f.at[c], pl.ds(0, WIDTH)
        n = chunks + c
        return n % 2, n, sib_i.at[c], pl.ds(0, 128)

    def pair_send(kind, c, op):
        s, n, sib, cols = chunk_refs(kind, c)
        copy = remote(grad.at[s, :, :, 1 - b, :, cols], sib, gs_ssem.at[n], gs_rsem.at[n], mate)
        if op == "start":
            copy.start()
        else:
            copy.wait_send()

    def line_refs(kind, c, side):
        if kind == "f":
            return (down_f if side else up_f).at[c], far_f.at[c]
        return (down_i if side else up_i).at[c], far_i.at[c]

    def line_range(side):
        return (0, o) if side else (o + 1, out_n)

    def line_send(kind, c, side, op="start"):
        _, n, _, _ = chunk_refs(kind, c)
        come, mine_far = line_refs(kind, c, side)
        rsem = (down_sem if side else up_sem)
        dev = (2 * (o + 1 - 2 * side) + a, g)

        def one(d, carry):
            copy = remote(mine_far.at[:, d], come.at[:, d], gz_ssem.at[n, d], rsem.at[n, d], dev)
            if op == "start":
                copy.start()
            else:
                copy.wait_send()
            return carry

        lax.fori_loop(*line_range(side), one, 0)

    def pair_sum(kind, c):
        s, n, sib, cols = chunk_refs(kind, c)
        _, mine_far = line_refs(kind, c, 0)
        await_bytes(sib, gs_rsem.at[n])
        fetch(sib, sibv.at[:, :, :, cols], 1)

        def one(i, carry):
            j, o2 = i // out_n, lax.rem(i, out_n)
            part[0, j, o2, :, cols] = (
                grad[s, j, o2, b, :, cols].astype(F32) + sibv[j, o2, :, cols].astype(F32)
            ).astype(BF)
            return carry

        lax.fori_loop(0, 3 * out_n, one, 0)
        fetch(part.at[0, :, :, :, cols], mine_far, 1)
        when(first, line_send, kind, c, 0)
        when(final, line_send, kind, c, 1)

    def line_step(kind, c, side):
        _, n, _, cols = chunk_refs(kind, c)
        come, mine_far = line_refs(kind, c, side)
        rsem = (down_sem if side else up_sem)
        low_d, high_d = line_range(side)
        await_bytes(come.at[:, o], rsem.at[n, o])

        def ask(d, carry):
            await_bytes(come.at[:, d], rsem.at[n, d])
            pltpu.make_async_copy(come.at[:, d], part.at[1, :, d, :, cols], lsem.at[3]).start()
            pltpu.make_async_copy(mine_far.at[:, d], sibv.at[:, d, :, cols], lsem.at[4]).start()
            pltpu.make_async_copy(come.at[:, d], part.at[1, :, d, :, cols], lsem.at[3]).wait()
            pltpu.make_async_copy(mine_far.at[:, d], sibv.at[:, d, :, cols], lsem.at[4]).wait()
            for j in range(3):
                sibv[j, d, :, cols] = (
                    sibv[j, d, :, cols].astype(F32) + part[1, j, d, :, cols].astype(F32)
                ).astype(BF)
            fetch(sibv.at[:, d, :, cols], mine_far.at[:, d], 1)
            return carry

        lax.fori_loop(low_d, high_d, ask, 0)
        when(jnp.logical_not(first if side else final), line_send, kind, c, side)

    def line_time(kind, time, number):
        for side, at in ((0, o), (1, out_n - 1 - o)):
            for c in [time - at] if kind == "f" else range(number):
                if kind == "f":
                    @pl.when((at > 0) & (c >= 0) & (c < number))
                    def _():
                        line_step(kind, c, side)
                else:
                    @pl.when((at > 0) & (c == time - at))
                    def _():
                        line_step(kind, c, side)

    def line_close(kind, c):
        when(jnp.logical_not(final), line_send, kind, c, 0, "end")
        when(jnp.logical_not(first), line_send, kind, c, 1, "end")

    def out_slot(n):
        return (n // (2 * out_n), slice(None), lax.rem(n, 2 * out_n) // 2, lax.rem(n, 2))

    def hand_back(kind, c, op):
        _, n, _, cols = chunk_refs(kind, c)
        dst = (g_ff if kind == "f" else g_wi)
        if not direct:
            if op == "start":
                h, _, o2, p = out_slot(n)
                fetch(ws.at[h, :, o2, p, :, cols], dst.at[c], 1)
            return
        h, _, o2, p = out_slot(n)
        for q in range(group):
            src = ws.at[h, :, o2, p, pl.ds(q * block, block), cols]
            switch(
                (a == b) & (q == g),
                pltpu.make_async_copy(src, dst.at[t, c], back_rsem.at[n, t]),
                remote(src, dst.at[t, c], back_ssem.at[n, q], back_rsem.at[n, t], (2 * o + b, q)),
                op,
            )

    def hand_wait(kind, c):
        if direct:
            _, n, _, _ = chunk_refs(kind, c)
            for t2 in range(group):
                await_bytes((g_ff if kind == "f" else g_wi).at[t2, c], back_rsem.at[n, t2])

    def total(kind, c):
        s, n, _, cols = chunk_refs(kind, c)
        h, _, place_o, place_p = out_slot(n)
        come_up, mine_far = line_refs(kind, c, 0)
        come_down, _ = line_refs(kind, c, 1)
        fetch(mine_far.at[:, o], sibv.at[:, 0, :, cols], 1)
        for m, (missing, come) in enumerate(((first, come_up), (final, come_down))):
            @pl.when(missing)
            def _(m=m):
                for j in range(3):
                    part[1, j, m, :, cols] = jnp.zeros((rows_n, 128 if kind == "i" else WIDTH), BF)

            @pl.when(jnp.logical_not(missing))
            def _(m=m, come=come):
                fetch(come.at[:, o], part.at[1, :, m, :, cols], 1)

        def add(i, carry):
            j = i // (rows_n // 48)
            here = pl.ds(pl.multiple_of(lax.rem(i, rows_n // 48) * 48, 16), 48)
            value = sibv[j, 0, here, cols].astype(F32)
            for m in range(2):
                value = value + part[1, j, m, here, cols].astype(F32)
            ws[h, j, place_o, place_p, here, cols] = value.astype(BF)
            return carry

        lax.fori_loop(0, 3 * (rows_n // 48), add, 0)
        hand_back(kind, c, "start")

    half = out_n // 2

    def grad_rows(h):
        return pl.ds(pl.multiple_of(h * (D // 2), D // 2), D // 2), pl.ds(h * half, half)

    loop_pump = out_n + 5

    def hidden_chunk(c, carry):
        s = lax.rem(c, 2)
        await_bytes(ws.at[s], wsem.at[s])
        hid, dgt, dup = (pl.ds(j * WIDTH, WIDTH) for j in range(3))

        def token_tile(m, carry):
            here = pl.ds(pl.multiple_of(m * (seq // 2), seq // 2), seq // 2)
            n2 = act[here, :]
            gate = dot(n2, ws[s, 0].reshape(D, WIDTH))
            upper = dot(n2, ws[s, 1].reshape(D, WIDTH))
            d_hidden = dot(bck[here, :], ws[s, 2].reshape(D, WIDTH))
            sigma = jax.nn.sigmoid(gate)
            active = gate * sigma
            dmix[here, hid] = (active * upper).astype(BF)
            dmix[here, dgt] = (d_hidden * upper * (sigma * (1.0 + gate * (1.0 - sigma)))).astype(BF)
            dmix[here, dup] = (d_hidden * active).astype(BF)
            acc_y[here, :] += dot_t(dmix[here, hid], ws[s, 2].reshape(D, WIDTH))
            acc_n[here, :] += dot_t(dmix[here, dgt], ws[s, 0].reshape(D, WIDTH))
            acc_n[here, :] += dot_t(dmix[here, dup], ws[s, 1].reshape(D, WIDTH))
            return carry

        lax.fori_loop(0, 2, token_tile, 0)

        @pl.when(c >= 2)
        def _():
            pair_send("f", c - 2, "end")

        def grad_tile(h, carry):
            rows, os = grad_rows(h)
            shape = (half, 2, rows_n, WIDTH)
            grad[s, 0, os] = dot(act_t[rows, :], dmix[:, dgt]).astype(BF).reshape(shape)
            grad[s, 1, os] = dot(act_t[rows, :], dmix[:, dup]).astype(BF).reshape(shape)
            grad[s, 2, os] = dot(bck_t[rows, :], dmix[:, hid]).astype(BF).reshape(shape)
            return carry

        lax.fori_loop(0, 2, grad_tile, 0)
        pair_send("f", c, "start")

        @pl.when(c >= 1)
        def _():
            pair_sum("f", c - 1)

        pump(c + loop_pump)

        @pl.when(c + 1 < chunks)
        def _():
            gather_wait(c + 3)
            pltpu.make_async_copy(wf_all.at[c + 1], ws.at[1 - s], wsem.at[1 - s]).start()

        return carry

    lax.fori_loop(0, chunks, hidden_chunk, 0)

    def d_normed_two(q):
        stage[q] = acc_n[any_span(q), :].astype(BF)

    scatter(staged, rs_n2, 1, d_normed_two)
    pair_sum("f", chunks - 1)
    scatter_on(staged, rs_n2, 1)
    for time in range(1, 4):
        line_time("f", time, chunks)
    scatter_wait(rs_n2, 1)
    scatter_end(staged, rs_n2, 1)
    spread(low, n2_all, 2, "end")
    fetch(rs_n2, stage.at[pl.ds(0, 3)], 0)
    fetch(bck_own, act.at[span(0)], 0)
    g_gains[...] = jnp.zeros_like(g_gains)

    def d_middle_rows(i, carry):
        here = rows16(i)
        dn = arrived(here)
        mi = mid[here, :]
        s2 = lax.rsqrt(jnp.mean(mi * mi, axis=-1, keepdims=True) + EPS_NORM)
        e2 = gains[1:2, :] * dn
        back = act[here, :].astype(F32)
        dm = back + s2 * e2 - mi * (s2 * s2 * s2) * jnp.mean(e2 * mi, axis=-1, keepdims=True)
        dmid[here, :] = dm
        low[here, :] = dm.astype(BF)
        g_gains[1] += jnp.sum((dn * mi * s2).reshape(ROW_TILE // 8, 8, D), axis=0)
        return carry

    lax.fori_loop(0, seg // ROW_TILE, d_middle_rows, 0)
    spread(low, dbr_all, 3, "start")

    for q in range(group):
        stage[q] = acc_y[span(q), :].astype(BF)
    spill_back = pltpu.make_async_copy(mixed_far, acc_y.at[:, pl.ds(0, 3 * ch)], lsem.at[2])
    spill_back.start()

    for q in range(group):
        bck_t[pl.ds(0, ch), span(q)] = gated[span(q), :].T
        fetch(nrm_far.at[span(q)], act.at[span(q)], 0)
        act_t[:, span(q)] = act[span(q), :].T
    spill_back.wait()
    spread_on(dbr_all, 3)
    for time in range(4, 7):
        line_time("f", time, chunks)

    acc_n[pl.ds(seq, 8), pl.ds(0, ch)] = jnp.zeros((8, ch), F32)
    for q in range(group):
        spread_wait(dbr_all, 3, q)
        fetch(dbr_all.at[q], bck.at[span(q)], 0)
        acc_n[span(q), pl.ds(ch, ch)] = dot_t(bck[span(q), :], wo[...].reshape(ch, D))
        for k in range(blocks):
            col = pl.ds(k * 128, 128)
            d_gated = acc_n[span(q), pl.ds(ch + k * 128, 128)]
            acc_n[span(q), col] = d_gated * acc_y[span(q), lanes(k, 1)]
            dmix[span(q), lanes(k, 1)] = (d_gated * convolved(q, col)).astype(BF)
    scatter(staged, rs_y, 2, lambda q: None)
    g_taps[...] = jnp.zeros_like(g_taps)
    for q in range(group):
        for k in range(blocks):
            col = pl.ds(k * 128, 128)
            d0 = acc_n[span(q), col]
            for n in range(3):
                g_taps[n, :, col] += jnp.sum(
                    (d0 * prod[pl.ds(q * seg + 6 + n, seg), col]).reshape(seg // 8, 8, 128), axis=0
                )
            d_product = (
                taps[2:3, col] * d0
                + taps[1:2, col] * acc_n[pl.ds(q * seg + 1, seg), col]
                + taps[0:1, col] * acc_n[pl.ds(q * seg + 2, seg), col]
            )
            dmix[span(q), lanes(k, 0)] = (d_product * acc_y[span(q), lanes(k, 2)]).astype(BF)
            dmix[span(q), lanes(k, 2)] = (d_product * acc_y[span(q), lanes(k, 0)]).astype(BF)

    for k in range(blocks):
        s = (chunks + k) % 2
        if k < 2:
            pair_send("f", chunks - 2 + k, "end")
        else:
            pair_send("i", k - 2, "end")

        def intake_tile(h, carry, k=k, s=s):
            rows, os = grad_rows(h)
            value = dot(act_t[rows, :], dmix[:, pl.ds(k * 384, 384)]).astype(BF)
            for j in range(3):
                grad[s, j, os, :, :, pl.ds(0, 128)] = value[:, j * 128 : (j + 1) * 128].reshape(
                    half, 2, rows_n, 128
                )
            return carry

        lax.fori_loop(0, 2, intake_tile, 0)
        pair_send("i", k, "start")
        if k >= 1:
            pair_sum("i", k - 1)

    for n in range(4):
        col = pl.ds(n * 384, 384)
        wo[:, :, :, col] = dot(bck_t[pl.ds(0, ch), :], bck[:, col]).astype(BF).reshape(out_n, 2, cblk, 384)
    last = chunks + blocks
    pair_o = remote(wo.at[:, 1 - b], sib_o, gs_ssem.at[last], gs_rsem.at[last], mate)
    pair_o.start()
    pair_sum("i", blocks - 1)

    await_bytes(sib_o, gs_rsem.at[last])
    fetch(sib_o, sibo, 1)

    def add_o(o2, carry):
        parto[o2] = (wo[o2, b].astype(F32) + sibo[o2].astype(F32)).astype(BF)
        return carry

    lax.fori_loop(0, out_n, add_o, 0)

    def part_o(op):
        def one(k, carry):
            o2, dev = peer(k)
            copy = remote(parto.at[o2], z_o.at[o], gz_ssem.at[last, k], up_sem.at[last, o], dev)
            if op == "start":
                copy.start()
            else:
                copy.wait_send()
            return carry

        lax.fori_loop(1, out_n, one, 0)
        keep = pltpu.make_async_copy(parto.at[o], z_o.at[o], osem.at[0])
        if op == "start":
            keep.start()
        else:
            keep.wait()

    part_o("start")

    def lent(q):
        return bck.at[any_span(q)]

    def d_normed(q):
        for n in range(4):
            bck[any_span(q), pl.ds(n * 384, 384)] = dot_t(
                dmix[any_span(q), :], wi[pl.ds(n * out_n // 4, out_n // 4)].reshape(384, 3 * ch)
            ).astype(BF)

    scatter(lent, rs_n1, 3, d_normed)
    scatter_on(staged, rs_y, 2)
    scatter_on(lent, rs_n1, 3)
    scatter_wait(rs_y, 2)
    scatter_end(staged, rs_y, 2)
    spread(low, dbr_all, 3, "end")
    for q in range(3):
        fetch(rs_y.at[q], act.at[span(q)], 0)

    def out_rows(i, carry):
        here = rows16(i)
        value = act[here, :].astype(F32)
        for q in range(1, 3):
            value = value + act[pl.ds(pl.multiple_of(q * seg + i * ROW_TILE, ROW_TILE), ROW_TILE), :].astype(F32)
        low[here, :] = (mid[here, :] + value).astype(BF)
        return carry

    lax.fori_loop(0, seg // ROW_TILE, out_rows, 0)
    fetch(low, block_out, 0)

    for time in range(7, chunks + out_n - 1):
        line_time("f", time, chunks)

    def total_f(c, carry):
        total("f", c)
        return carry

    lax.fori_loop(0, chunks, total_f, 0)
    scatter_wait(rs_n1, 3)
    scatter_end(lent, rs_n1, 3)
    fetch(rs_n1, stage.at[pl.ds(0, 3)], 0)

    def d_rows(i, carry):
        here = rows16(i)
        dn = arrived(here)
        row = tok[here, :].astype(F32)
        s1 = lax.rsqrt(jnp.mean(row * row, axis=-1, keepdims=True) + EPS_NORM)
        e1 = gains[0:1, :] * dn
        low[here, :] = (
            dmid[here, :] + s1 * e1 - row * (s1 * s1 * s1) * jnp.mean(e1 * row, axis=-1, keepdims=True)
        ).astype(BF)
        g_gains[0] += jnp.sum((dn * row * s1).reshape(ROW_TILE // 8, 8, D), axis=0)
        return carry

    lax.fori_loop(0, seg // ROW_TILE, d_rows, 0)
    fetch(low, input_grad, 0)

    sm_mine[...] = jnp.zeros_like(sm_mine)
    for i in range(2):
        value = jnp.sum(g_gains[i], axis=0, keepdims=True)
        for j in range(D // 128):
            row = i * (D // 128) + j
            sm_mine[row : row + 1, :] = value[:, j * 128 : (j + 1) * 128]
    for n in range(3):
        value = jnp.sum(g_taps[n], axis=0, keepdims=True)
        for k in range(blocks):
            for t2 in range(group):
                row = 2 * (D // 128) + (t2 * 3 + n) * blocks + k
                sm_mine[row : row + 1, :] = jnp.where(t == t2, value[:, k * 128 : (k + 1) * 128], 0.0)
    sm_plane[place] = sm_mine[...]
    plane(sm_mine, sm_plane.at[place], ta_ssem, ta_rsem, "start")

    for k in range(max(0, blocks - 2), blocks):
        pair_send("i", k, "end")

    def lines(time, carry):
        line_time("i", time, blocks)
        return carry

    lax.fori_loop(1, out_n - 1, lines, 0)
    plane_wait(sm_mine, ta_rsem)
    value = sm_plane[0]
    for i in range(1, 2 * group):
        value = value + sm_plane[i]
    sm_sum[...] = value
    sm_z[o] = value
    far(sm_sum, sm_z.at[o], tz_ssem, tz_rsem, "start")
    lax.fori_loop(out_n - 1, blocks + out_n - 1, lines, 0)
    for k in range(blocks):
        total("i", k)
    part_o("end")
    pair_o.wait_send()

    def last_one(k, carry):
        await_bytes(z_o.at[o], up_sem.at[last, peer(k)[0]])
        return carry

    lax.fori_loop(1, out_n, last_one, 0)
    fetch(z_o, sibo, 1)
    value = sibo[0].astype(F32)
    for o2 in range(1, out_n):
        value = value + sibo[o2].astype(F32)
    outo = parto.at[0]
    outo[...] = value.astype(BF)

    def back_o(op):
        switch(
            a == b,
            pltpu.make_async_copy(outo, g_wo, back_rsem.at[last, 0]),
            remote(outo, g_wo, back_ssem.at[last, 0], back_rsem.at[last, 0], (2 * o + b, 2 * y + a)),
            op,
        )

    back_o("start")
    far_wait(sm_sum, tz_rsem)
    value = sm_z[0]
    for i in range(1, out_n):
        value = value + sm_z[i]
    g_small[...] = value

    plane(small_own, small_all.at[mine], sa_ssem, sa_rsem, "end")
    far(planes, planes, sz_ssem, sz_rsem, "end")
    plane(sm_mine, sm_plane.at[place], ta_ssem, ta_rsem, "end")
    far(sm_sum, sm_z.at[o], tz_ssem, tz_rsem, "end")
    spread(tok, tok_all, 0, "end")
    spread(bck_own, bck_all, 1, "end")
    gather_close(0)
    gather_close(1)

    def close(c, carry):
        gather_close(c + 2)
        line_close("f", c)
        hand_back("f", c, "end")
        hand_wait("f", c)
        return carry

    lax.fori_loop(0, chunks, close, 0)
    for k in range(blocks):
        line_close("i", k)
        hand_back("i", k, "end")
        hand_wait("i", k)
    back_o("end")
    await_bytes(g_wo, back_rsem.at[last, 0])


def forward_backward(sizes, tok, bck, wi_own, wo_own, ff_own, small_own):
    (out_n, group, rows_n, seg, ch, cblk, chunks) = sizes
    blocks = ch // 128
    seq = group * seg
    block = rows_n // group
    places = 2 * group
    small_rows = -(-(2 * D // 128 + group * 3 * blocks) // 8) * 8
    items = 2 + chunks
    sums = chunks + blocks + 1
    vm = pltpu.VMEM
    dma = pltpu.SemaphoreType.DMA

    def shape(*dims, dtype=BF):
        return jax.ShapeDtypeStruct(dims, dtype)

    any_spec = pl.BlockSpec(memory_space=pl.ANY)
    vmem_spec = pl.BlockSpec(memory_space=pltpu.VMEM)
    if block % 16 == 0:
        given = [shape(group, chunks, 3, block, WIDTH), shape(group, blocks, 3, block, 128)]
    else:
        given = [shape(chunks, 3, rows_n, WIDTH), shape(blocks, 3, rows_n, 128)]
    outs = [
        shape(seg, D), shape(seg, D), *given, shape(cblk, D), shape(small_rows, 128, dtype=F32),
        shape(chunks, 3, out_n, 2, rows_n, WIDTH), shape(out_n, 2, rows_n, 3 * ch), shape(out_n, 2, cblk, D),
        shape(group, seg, D), shape(seq, D), shape(group, seg, D), shape(group, seg, D), shape(group, seg, D),
        shape(3, seg, D), shape(3, seg, D), shape(3, seg, D), shape(3, seg, D), shape(4, 2, seg // 2, D),
        shape(chunks, 3, out_n, rows_n, WIDTH), shape(blocks, 3, out_n, rows_n, 128), shape(out_n, cblk, D),
        *[shape(chunks, 3, out_n, rows_n, WIDTH), shape(blocks, 3, out_n, rows_n, 128)] * 3, shape(out_n, cblk, D),
        shape(seq, 3 * ch, dtype=F32),
    ]
    out_specs = [any_spec] * 5 + [vmem_spec] + [any_spec] * (len(outs) - 6)
    scratch = [
        vm((2, 3, out_n, 2, rows_n, WIDTH), BF),
        vm((out_n, 2, rows_n, 3 * ch), BF),
        vm((out_n, 2, cblk, D), BF),
        vm((seq, D), BF), vm((D, seq), BF), vm((seq, D), BF), vm((D, seq), BF),
        vm((seq, D), F32), vm((seq + 8, D), F32),
        vm((2, 3, out_n, 2, rows_n, WIDTH), BF),
        vm((3, out_n, rows_n, WIDTH), BF),
        vm((2, 3, out_n, rows_n, WIDTH), BF),
        vm((group, seg, D), BF),
        vm((seq + 8, ch), F32), vm((seq, ch), BF), vm((seq, 3 * ch), BF),
        vm((seg, D), F32), vm((seg, D), F32), vm((seg, D), BF),
        vm((out_n, cblk, D), BF), vm((out_n, cblk, D), BF),
        vm((places * out_n, 8, 128), F32), vm((2, D), F32), vm((3, ch), F32),
        vm((2, 8, D), F32), vm((3, 8, ch), F32),
        vm((small_rows, 128), F32), vm((places, small_rows, 128), F32),
        vm((small_rows, 128), F32), vm((out_n, small_rows, 128), F32),
        vm((seg // 2, D), BF),
        dma((4, 3, 2)), dma((4, group, 2)), dma((4, 2)), dma((4, 4, 2)), dma((4, 3, 2)), dma((4, 2, 2)), dma((4, 2)),
        dma((items, 2, out_n)), dma((items, out_n)), dma((items,)), dma((items,)),
        dma((sums,)), dma((sums,)), dma((sums, out_n)), dma((sums, out_n)), dma((sums, out_n)),
        dma((items, group)), dma((items, group)), dma((sums, group)), dma((sums, group)), dma((1,)),
        dma((places,)), dma((places,)), dma((out_n,)), dma((out_n,)),
        dma((places,)), dma((places,)), dma((out_n,)), dma((out_n,)), dma((2,)), dma((5,)),
    ]
    results = pl.pallas_call(
        functools.partial(block_kernel, sizes),
        out_shape=outs,
        in_specs=[vmem_spec] + [any_spec] * 4 + [vmem_spec],
        out_specs=out_specs,
        scratch_shapes=scratch,
        compiler_params=pltpu.CompilerParams(
            collective_id=0, has_side_effects=True, vmem_limit_bytes=63 * 1024 * 1024
        ),
        cost_estimate=pl.CostEstimate(
            flops=6 * seq * D * (4 * ch + 3 * chunks * WIDTH),
            bytes_accessed=200_000_000,
            transcendentals=seq * chunks * WIDTH,
        ),
    )(tok, bck, wi_own, wo_own, ff_own, small_own)
    return results[:6]


def body(
    tokens,
    cotangent,
    lengths,
    intake_weight,
    intake_first,
    intake_second,
    output_weight,
    output_first,
    output_second,
    swiglu_weight,
    swiglu_first,
    swiglu_second,
    down_weight,
    down_first,
    down_second,
    norm_gains,
    gains_first,
    gains_second,
    conv_kernel,
    kernel_first,
    kernel_second,
):
    data_count = lax.axis_size("dp")
    group_count = lax.axis_size("group")
    dp = lax.axis_index("dp")
    member = lax.axis_index("group")
    block = D // (data_count * group_count)
    cblk = -(-block // 16) * 16
    ch = data_count * cblk
    blocks = ch // 128
    hidden_part = FF // group_count
    chunks = -(-hidden_part // WIDTH)
    hidden_full = chunks * WIDTH
    rows_n = D // data_count
    swap = []
    for one in range(data_count):
        for two in range(group_count):
            there = (2 * (one // 2) + two % 2) * group_count + 2 * (two // 2) + one % 2
            swap.append((one * group_count + two, there))

    def cross(value):
        return lax.ppermute(value, ("dp", "group"), swap)

    intake_local = (
        intake_weight.astype(BF)
        .reshape(block, 3, data_count, group_count, block)
        .transpose(3, 0, 1, 2, 4)
    )
    intake_local = jnp.pad(intake_local, ((0, 0),) * 4 + ((0, cblk - block),))
    intake_local = (
        intake_local.reshape(group_count, block, 3, blocks, 128)
        .transpose(0, 1, 3, 2, 4)
        .reshape(group_count, block, 3 * ch)
    )
    ff_local = jnp.concatenate(
        [
            swiglu_weight.astype(BF).reshape(block, 2, group_count, hidden_part),
            down_weight.astype(BF).reshape(block, 1, group_count, hidden_part),
        ],
        axis=1,
    )
    ff_local = jnp.pad(ff_local, ((0, 0),) * 3 + ((0, hidden_full - hidden_part),))
    ff_local = ff_local.reshape(block, 3, group_count, chunks, WIDTH).transpose(2, 3, 1, 0, 4)
    wo_own = jnp.pad(output_weight.astype(BF).reshape(block, D), ((0, cblk - block), (0, 0)))
    if block % 16 == 0:
        wi_own, ff_own = intake_local, ff_local
    else:
        wi_own = lax.all_to_all(intake_local, "group", split_axis=0, concat_axis=0, tiled=True)
        wi_own = cross(wi_own.reshape(rows_n, 3 * ch))
        ff_own = lax.all_to_all(ff_local, "group", split_axis=0, concat_axis=0, tiled=True)
        ff_own = cross(ff_own.transpose(1, 2, 0, 3, 4).reshape(chunks, 3, rows_n, WIDTH))

    number = dp * group_count + member
    share = norm_gains.shape[0]

    def placed(values, lane):
        line = lax.dynamic_update_slice(jnp.zeros((256,), F32), lax.reduce_precision(values, 8, 7), (lane,))
        return line.reshape(2, 128)

    runs = [placed(norm_gains, lax.rem(number * share, 128))]
    for piece in range(3):
        rest = lax.rem(3 * number + piece, data_count * group_count)
        lane = lax.rem(rest // group_count * cblk, 128)
        runs.append(placed(conv_kernel[piece * block : (piece + 1) * block], lane))
    small_own = jnp.concatenate(runs)

    seg_len = tokens.shape[1]
    positions = member * seg_len + lax.iota(jnp.int32, seg_len)
    valid = (positions < lengths[0]).astype(F32)[:, None]
    back_low = (cotangent[0].astype(F32) * valid).astype(BF)

    sizes = (data_count // 2, group_count, rows_n, seg_len, ch, cblk, chunks)
    block_out, input_grad, g_ff, g_wi, g_wo, g_small = forward_backward(
        sizes, tokens[0], back_low, wi_own, wo_own, ff_own, small_own
    )

    if block % 16:
        g_wi = cross(g_wi).reshape(blocks, 3, group_count, block, 128).transpose(2, 0, 1, 3, 4)
        g_wi = lax.all_to_all(g_wi, "group", split_axis=0, concat_axis=0, tiled=True)
        g_ff = cross(g_ff).reshape(chunks, 3, group_count, block, WIDTH).transpose(2, 0, 1, 3, 4)
        g_ff = lax.all_to_all(g_ff, "group", split_axis=0, concat_axis=0, tiled=True)
    g_wi = g_wi.transpose(0, 3, 2, 1, 4).reshape(group_count, block, 3, data_count, cblk)
    intake_grad_flat = g_wi[..., :block].transpose(1, 2, 3, 0, 4).reshape(-1).astype(F32)
    g_ff = g_ff.transpose(3, 2, 0, 1, 4).reshape(block, 3, group_count, hidden_full)
    g_ff = g_ff[..., :hidden_part]
    swiglu_grad_flat = g_ff[:, :2].reshape(-1).astype(F32)
    down_grad_flat = g_ff[:, 2].reshape(-1).astype(F32)
    output_grad_flat = g_wo[:block].reshape(-1).astype(F32)

    gain_rows = 2 * D // 128
    taps_grad = g_small[gain_rows : gain_rows + group_count * 3 * blocks]
    taps_grad = taps_grad.reshape(group_count, 3, data_count, cblk)[..., :block]
    taps_grad = taps_grad.transpose(1, 2, 0, 3).reshape(-1)
    small_shards = (
        lax.dynamic_slice(g_small[:gain_rows].reshape(-1), (number * share,), (share,)),
        lax.dynamic_slice(taps_grad, (number * 3 * block,), (3 * block,)),
    )
    intake_new = update(
        intake_weight, intake_first, intake_second, intake_grad_flat, RATE_MATRIX, DECAY
    )
    output_new = update(
        output_weight, output_first, output_second, output_grad_flat, RATE_MATRIX, DECAY
    )
    swiglu_new = update(
        swiglu_weight, swiglu_first, swiglu_second, swiglu_grad_flat, RATE_MATRIX, DECAY
    )
    down_new = update(down_weight, down_first, down_second, down_grad_flat, RATE_MATRIX, DECAY)
    gains_new = update(norm_gains, gains_first, gains_second, small_shards[0], RATE_VECTOR, 0.0)
    kernel_new = update(
        conv_kernel, kernel_first, kernel_second, small_shards[1], RATE_VECTOR, DECAY
    )
    return (
        block_out[None],
        input_grad[None],
        intake_new[0],
        intake_new[1],
        intake_new[2],
        output_new[0],
        output_new[1],
        output_new[2],
        swiglu_new[0],
        swiglu_new[1],
        swiglu_new[2],
        down_new[0],
        down_new[1],
        down_new[2],
        gains_new[0],
        gains_new[1],
        gains_new[2],
        kernel_new[0],
        kernel_new[1],
        kernel_new[2],
    )


def solution(mesh):
    in_specs = (
        P("dp", "group", None),
        P("dp", "group", None),
        P("dp"),
        P(("dp", "group")),
        P(("dp", "group")),
        P(("dp", "group")),
        P(("dp", "group")),
        P(("dp", "group")),
        P(("dp", "group")),
        P(("dp", "group")),
        P(("dp", "group")),
        P(("dp", "group")),
        P(("dp", "group")),
        P(("dp", "group")),
        P(("dp", "group")),
        P(("dp", "group")),
        P(("dp", "group")),
        P(("dp", "group")),
        P(("dp", "group")),
        P(("dp", "group")),
        P(("dp", "group")),
    )
    out_specs = (
        P("dp", "group", None),
        P("dp", "group", None),
        P(("dp", "group")),
        P(("dp", "group")),
        P(("dp", "group")),
        P(("dp", "group")),
        P(("dp", "group")),
        P(("dp", "group")),
        P(("dp", "group")),
        P(("dp", "group")),
        P(("dp", "group")),
        P(("dp", "group")),
        P(("dp", "group")),
        P(("dp", "group")),
        P(("dp", "group")),
        P(("dp", "group")),
        P(("dp", "group")),
        P(("dp", "group")),
        P(("dp", "group")),
        P(("dp", "group")),
    )
    return jax.shard_map(body, mesh=mesh, in_specs=in_specs, out_specs=out_specs, check_vma=False)
```

profile of v0, /device:TPU:1, one launch (start us, length us, event | category | flops | bytes accessed | tf_op | source)
XLA Modules:
  0.0 600.1 jit_solution(2878736921446595522)
XLA Ops:
  0.7 0.0 copy-start.4
  1.5 0.8 reduce-precision_dynamic-update-slice_fusion.2
  2.3 0.8 reduce-precision_dynamic-update-slice_fusion.1
  3.2 0.8 reduce-precision_dynamic-update-slice_fusion
  4.0 0.7 reduce-precision_dynamic-update-slice_fusion.3
  4.7 0.6 pad_maximum_fusion.small_own
  5.3 1.0 convert_element_type.68
  6.3 0.9 reshape.110.wo_own
  7.2 1.2 convert_element_type.67
  8.4 0.1 convert_element_type.70
  8.5 0.7 reshape.112
  9.2 1.0 reshape.107
  10.2 0.2 copy.47
  10.4 1.6 reshape.108
  11.9 2.3 copy.48
  14.3 2.1 reshape.109.wi_own
  16.4 2.2 fusion.4.bck_own
  18.6 1.2 convert_element_type.69
  19.8 3.4 reshape.111
  23.2 2.0 fusion.3
  25.2 4.0 reshape.128
  29.2 2.6 copy.62
  31.8 0.0 copy-start.17
  31.8 0.0 copy-start.18
  31.8 0.0 copy-start.8
  31.8 0.0 copy-start.14
  31.9 0.0 copy-start.15
  31.9 522.3 %shard_map.356 = (bf16[256,1536]{1,0:T(8,128)(2,1)}, bf16[256,1536]{1,0:T(8,128)(2,1)}, bf16[4,7,3,48,256]{4,3,2,1,0:T(8,128)(2,1)}, bf16[4,3,3,48,128]{4,3,2,1,...) custom-call(bf16[256,1536]{1,0:T(8,128)(2,1)} %bitcast.46, ...), custom_call_target="tpu_custom_call" | custom-call | flops 65229815808 | bytes 200000000 | tf_op jit(solution)/shard_map/pallas_call | solution.py:1107
  554.1 0.0 copy-start.13
  554.1 0.8 slice_bitcast_fusion
  554.9 0.7 slice.30
  555.6 0.0 copy-done.19
  555.6 0.0 copy-done.21
  555.6 0.6 multiply_subtract_fusion.5
  556.3 0.1 reshape.120
  556.4 0.1 reshape.121
  556.5 0.0 copy-done.16
  556.5 0.0 copy-done.17
  556.5 0.0 copy-done.18
  556.5 0.7 multiply_subtract_fusion.4
  557.2 1.1 reshape.124
  558.3 1.1 multiply_subtract_fusion.3
  559.3 0.1 convert_bitcast_fusion
  559.4 0.5 copy.52
  559.9 1.1 reshape.127
  561.0 2.9 copy.53
  563.9 3.6 reshape.123
  567.6 2.0 multiply_subtract_fusion.2
  569.6 0.3 copy-done.7
  569.9 0.9 copy.54
  570.8 3.5 reshape.118
  574.4 1.2 slice_convert_fusion.1
  575.6 0.0 copy-start.3
  575.6 0.9 copy.56
  576.5 2.2 reshape.126
  578.7 0.2 slice_convert_fusion
  578.9 1.8 copy.55
  580.7 3.8 reshape.125
  584.5 5.3 multiply_subtract_fusion.1
  589.8 1.1 copy-done.6
  590.8 6.5 %multiply_subtract_fusion = (f32[663552]{0:T(1024)}, f32[663552]{0:T(1024)}, f32[663552]{0:T(1024)}) fusion(f32[663552]{0:T(1024)S(1)} %copy-done.1, f32[663552]{0:T(1024)S(1)} %copy-done.2, f32[663552]{0:T(1024)S(1)} %copy-done.6, f32[663552]{0:T(1024)} %param.31), kind=kLoop, calls=%fused_computation.6 | loop fusion | flops 9289728 | bytes 18579456 | tf_op jit(solution)/shard_map/sub | solution.py:34
  597.3 0.9 copy.71
  598.2 0.5 copy-done.11
  598.7 0.9 copy.72
  (34 shorter events, 0.1 us)
Async XLA Ops:
  0.7 7.7 %copy-start.4 = (f32[331776]{0:T(1024)S(1)}, f32[331776]{0:T(1024)}, u32[]{:S(2)}) copy-start(f32[331776]{0:T(1024)} %param.33) | copy-start | bytes 3981316
  11.9 6.7 %copy-start = (f32[663552]{0:T(1024)S(1)}, f32[663552]{0:T(1024)}, u32[]{:S(2)}) copy-start(f32[663552]{0:T(1024)} %param.30) | copy-start | bytes 7962628
  31.8 523.8 %copy-start.19 = (f32[96]{0:T(128)S(1)}, f32[96]{0:T(128)}, u32[]{:S(2)}) copy-start(f32[96]{0:T(128)} %param.36) | copy-start | bytes 1156
  31.8 523.8 %copy-start.20 = (f32[96]{0:T(128)S(1)}, f32[96]{0:T(128)}, u32[]{:S(2)}) copy-start(f32[96]{0:T(128)} %param.38) | copy-start | bytes 1156
  31.8 523.8 %copy-start.21 = (f32[96]{0:T(128)S(1)}, f32[96]{0:T(128)}, u32[]{:S(2)}) copy-start(f32[96]{0:T(128)} %param.37) | copy-start | bytes 1156
  31.8 524.7 %copy-start.16 = (f32[144]{0:T(256)S(1)}, f32[144]{0:T(256)}, u32[]{:S(2)}) copy-start(f32[144]{0:T(256)} %param.39) | copy-start | bytes 1732
  31.8 524.7 %copy-start.17 = (f32[144]{0:T(256)S(1)}, f32[144]{0:T(256)}, u32[]{:S(2)}) copy-start(f32[144]{0:T(256)} %param.41) | copy-start | bytes 1732
  31.8 524.7 %copy-start.18 = (f32[144]{0:T(256)S(1)}, f32[144]{0:T(256)}, u32[]{:S(2)}) copy-start(f32[144]{0:T(256)} %param.40) | copy-start | bytes 1732
  31.8 526.4 %copy-start.8 = (f32[73728]{0:T(1024)S(1)}, f32[73728]{0:T(1024)}, u32[]{:S(2)}) copy-start(f32[73728]{0:T(1024)} %param.27) | copy-start | bytes 884740
  31.8 526.4 %copy-start.14 = (f32[73728]{0:T(1024)S(1)}, f32[73728]{0:T(1024)}, u32[]{:S(2)}) copy-start(f32[73728]{0:T(1024)} %param.29) | copy-start | bytes 884740
  31.9 526.4 %copy-start.15 = (f32[73728]{0:T(1024)S(1)}, f32[73728]{0:T(1024)}, u32[]{:S(2)}) copy-start(f32[73728]{0:T(1024)} %param.28) | copy-start | bytes 884740
  554.1 5.2 copy-start.13
  563.9 3.6 copy-start.5
  563.9 3.6 copy-start.9
  563.9 3.7 copy-start.10
  567.6 2.3 copy-start.7
  575.6 3.1 copy-start.3
  584.5 5.3 copy-start.1
  584.5 5.3 copy-start.2
  584.5 6.4 %copy-start.6 = (f32[663552]{0:T(1024)S(1)}, f32[663552]{0:T(1024)}, u32[]{:S(2)}) copy-start(f32[663552]{0:T(1024)} %param.32) | copy-start | bytes 7962628
  590.8 6.5 %copy-start.12 = (bf16[256,1536]{1,0:T(8,128)(2,1)S(1)}, bf16[256,1536]{1,0:T(8,128)(2,1)}, u32[]{:S(2)}) copy-start(bf16[256,1536]{1,0:T(8,128)(2,1)} %get-tuple-element.26) | copy-start | bytes 2359300
  597.3 1.4 copy-start.11
where the time goes:
time: 611 us; the launch traced here: 600 us
  Pallas kernels  522 us (85%)
  local copies, waits for them, and re-layouts  46.6 us (8%)
  other arithmetic  29 us (5%)
    pallas_call x1, Pallas kernels, forward_backward(): pl.pallas_call(functools.partial(block_kernel, sizes), out_shape=outs, in...  522 us
    sub x6, other arithmetic, update(): weight - rate * (first_hat / (jnp.sqrt(second_hat) + ADAM_EPS) + decay *...  16.1 us

commit v1 on v0

--- a/solution.py
+++ b/solution.py
@@ -53,12 +53,12 @@
     block_out, input_grad, g_ff, g_wi, g_wo, g_small,
     wf_all, wi_all, wo_all, tok_all, nrm_far, bck_all, n2_all, dbr_all,
     rs_br, rs_y, rs_n2, rs_n1, via,
-    sib_f, sib_i, sib_o, up_f, up_i, down_f, down_i, far_f, far_i, z_o, mixed_far,
+    sib_f, sib_i, sib_o, come_f, come_i, far_f, far_i, z_o, mixed_far,
     ws, wi, wo, act, act_t, bck, bck_t, acc_y, acc_n, grad, sibv, part, stage,
     prod, gated, dmix, mid, dmid, low, sibo, parto,
     small_all, gains, taps, g_gains, g_taps, sm_mine, sm_plane, sm_sum, sm_z,
     extra, ag_ssem, ag_rsem, ag_fsem, rs_ssem, rs_rsem, via_ssem, via_rsem, z_ssem, z_rsem, f_ssem, f_rsem,
-    gs_ssem, gs_rsem, gz_ssem, up_sem, down_sem, own_ssem, own_rsem, back_ssem, back_rsem, osem,
+    gs_ssem, gs_rsem, gz_ssem, come_sem, far_sem, buf_sem, own_ssem, own_rsem, back_ssem, back_rsem, osem,
     sa_ssem, sa_rsem, sz_ssem, sz_rsem, ta_ssem, ta_rsem, tz_ssem, tz_rsem, wsem, lsem,
 ):
     (out_n, group, rows_n, seg, ch, cblk, chunks) = sizes
@@ -578,86 +578,131 @@
         else:
             copy.wait_send()
 
-    def line_refs(kind, c, side):
-        if kind == "f":
-            return (down_f if side else up_f).at[c], far_f.at[c]
-        return (down_i if side else up_i).at[c], far_i.at[c]
-
-    def line_range(side):
-        return (0, o) if side else (o + 1, out_n)
-
-    def line_send(kind, c, side, op="start"):
+    steps = out_n.bit_length() - 1
+
+    def halves_refs(kind, c):
+        return (come_f if kind == "f" else come_i).at[c], (far_f if kind == "f" else far_i).at[c]
+
+    def flipped(k):
+        m = 1 << k
+        return o + m - 2 * m * lax.rem(o // m, 2)
+
+    def kept(device, k, i):
+        return lax.rem(device, 2 << k) + (2 << k) * i
+
+    def step_at(k):
+        return out_n - (out_n >> k), out_n >> (k + 1)
+
+    def step_send(kind, c, k, op="start"):
         _, n, _, _ = chunk_refs(kind, c)
-        come, mine_far = line_refs(kind, c, side)
-        rsem = (down_sem if side else up_sem)
-        dev = (2 * (o + 1 - 2 * side) + a, g)
-
-        def one(d, carry):
-            copy = remote(mine_far.at[:, d], come.at[:, d], gz_ssem.at[n, d], rsem.at[n, d], dev)
+        come, mine_far = halves_refs(kind, c)
+        at, number = step_at(k)
+        there = flipped(k)
+        for i in range(number):
+            copy = remote(
+                mine_far.at[:, kept(there, k, i)], come.at[:, at + i],
+                gz_ssem.at[n, at + i], come_sem.at[n, at + i], (2 * there + a, g),
+            )
             if op == "start":
                 copy.start()
             else:
                 copy.wait_send()
-            return carry
-
-        lax.fori_loop(*line_range(side), one, 0)
-
-    def pair_sum(kind, c):
+
+    def pair_fetch(kind, c, op):
         s, n, sib, cols = chunk_refs(kind, c)
-        _, mine_far = line_refs(kind, c, 0)
-        await_bytes(sib, gs_rsem.at[n])
-        fetch(sib, sibv.at[:, :, :, cols], 1)
+        if op == "start":
+            await_bytes(sib, gs_rsem.at[n])
+        copy = pltpu.make_async_copy(sib, sibv.at[:, :, :, cols], lsem.at[1])
+        copy.start() if op == "start" else copy.wait()
+
+    def pair_far(kind, c):
+        s, n, _, cols = chunk_refs(kind, c)
+        return pltpu.make_async_copy(part.at[s, :, :, :, cols], halves_refs(kind, c)[1], far_sem.at[s])
+
+    def pair_add(kind, c):
+        s, n, _, cols = chunk_refs(kind, c)
+        pair_fetch(kind, c, "end")
 
         def one(i, carry):
             j, o2 = i // out_n, lax.rem(i, out_n)
-            part[0, j, o2, :, cols] = (
+            part[s, j, o2, :, cols] = (
                 grad[s, j, o2, b, :, cols].astype(F32) + sibv[j, o2, :, cols].astype(F32)
             ).astype(BF)
             return carry
 
         lax.fori_loop(0, 3 * out_n, one, 0)
-        fetch(part.at[0, :, :, :, cols], mine_far, 1)
-        when(first, line_send, kind, c, 0)
-        when(final, line_send, kind, c, 1)
-
-    def line_step(kind, c, side):
+        pair_far(kind, c).start()
+
+    def first_send(kind, c):
+        pair_far(kind, c).wait()
+        step_send(kind, c, 0)
+
+    def stage_ask(job, buf, op):
+        kind, c, k = job
         _, n, _, cols = chunk_refs(kind, c)
-        come, mine_far = line_refs(kind, c, side)
-        rsem = (down_sem if side else up_sem)
-        low_d, high_d = line_range(side)
-        await_bytes(come.at[:, o], rsem.at[n, o])
-
-        def ask(d, carry):
-            await_bytes(come.at[:, d], rsem.at[n, d])
-            pltpu.make_async_copy(come.at[:, d], part.at[1, :, d, :, cols], lsem.at[3]).start()
-            pltpu.make_async_copy(mine_far.at[:, d], sibv.at[:, d, :, cols], lsem.at[4]).start()
-            pltpu.make_async_copy(come.at[:, d], part.at[1, :, d, :, cols], lsem.at[3]).wait()
-            pltpu.make_async_copy(mine_far.at[:, d], sibv.at[:, d, :, cols], lsem.at[4]).wait()
-            for j in range(3):
-                sibv[j, d, :, cols] = (
-                    sibv[j, d, :, cols].astype(F32) + part[1, j, d, :, cols].astype(F32)
+        come, mine_far = halves_refs(kind, c)
+        at, number = step_at(k)
+        for i in range(number):
+            if op == "start":
+                await_bytes(come.at[:, at + i], come_sem.at[n, at + i])
+            for m, src in ((i, come.at[:, at + i]), (number + i, mine_far.at[:, kept(o, k, i)])):
+                copy = pltpu.make_async_copy(src, part.at[buf, :, m, :, cols], buf_sem.at[buf, m])
+                copy.start() if op == "start" else copy.wait()
+
+    def stage_back(job, buf, op):
+        kind, c, k = job
+        _, n, _, cols = chunk_refs(kind, c)
+        mine_far = halves_refs(kind, c)[1]
+        at, number = step_at(k)
+        for i in range(number):
+            m = number + i
+            copy = pltpu.make_async_copy(
+                part.at[buf, :, m, :, cols], mine_far.at[:, kept(o, k, i)], buf_sem.at[buf, m]
+            )
+            copy.start() if op == "start" else copy.wait()
+
+    def stage_add(job, buf):
+        kind, c, k = job
+        _, n, _, cols = chunk_refs(kind, c)
+        h, _, place_o, place_p = out_slot(n)
+        at, number = step_at(k)
+
+        def add(i, carry):
+            j, r = i // (rows_n // 48), lax.rem(i, rows_n // 48)
+            here = pl.ds(pl.multiple_of(r * 48, 16), 48)
+            for m in range(number):
+                value = (
+                    part[buf, j, m, here, cols].astype(F32) + part[buf, j, number + m, here, cols].astype(F32)
                 ).astype(BF)
-            fetch(sibv.at[:, d, :, cols], mine_far.at[:, d], 1)
+                if k == steps - 1:
+                    ws[h, j, place_o, place_p, here, cols] = value
+                else:
+                    part[buf, j, number + m, here, cols] = value
             return carry
 
-        lax.fori_loop(low_d, high_d, ask, 0)
-        when(jnp.logical_not(first if side else final), line_send, kind, c, side)
-
-    def line_time(kind, time, number):
-        for side, at in ((0, o), (1, out_n - 1 - o)):
-            for c in [time - at] if kind == "f" else range(number):
-                if kind == "f":
-                    @pl.when((at > 0) & (c >= 0) & (c < number))
-                    def _():
-                        line_step(kind, c, side)
-                else:
-                    @pl.when((at > 0) & (c == time - at))
-                    def _():
-                        line_step(kind, c, side)
-
-    def line_close(kind, c):
-        when(jnp.logical_not(final), line_send, kind, c, 0, "end")
-        when(jnp.logical_not(first), line_send, kind, c, 1, "end")
+        lax.fori_loop(0, 3 * (rows_n // 48), add, 0)
+        if k == steps - 1:
+            hand_back(kind, c, "start")
+        else:
+            stage_back(job, buf, "start")
+
+    def stage_on(job, buf):
+        kind, c, k = job
+        if k < steps - 1:
+            stage_back(job, buf, "end")
+            step_send(kind, c, k + 1)
+
+    def sums_of(jobs):
+        for i, job in enumerate(jobs):
+            if i == 0:
+                stage_ask(job, 0, "start")
+            if i >= 1:
+                stage_on(jobs[i - 1], (i - 1) % 2)
+            if i + 1 < len(jobs):
+                stage_ask(jobs[i + 1], (i + 1) % 2, "start")
+            stage_ask(job, i % 2, "end")
+            stage_add(job, i % 2)
+        stage_on(jobs[-1], (len(jobs) - 1) % 2)
 
     def out_slot(n):
         return (n // (2 * out_n), slice(None), lax.rem(n, 2 * out_n) // 2, lax.rem(n, 2))
@@ -686,34 +731,6 @@
             for t2 in range(group):
                 await_bytes((g_ff if kind == "f" else g_wi).at[t2, c], back_rsem.at[n, t2])
 
-    def total(kind, c):
-        s, n, _, cols = chunk_refs(kind, c)
-        h, _, place_o, place_p = out_slot(n)
-        come_up, mine_far = line_refs(kind, c, 0)
-        come_down, _ = line_refs(kind, c, 1)
-        fetch(mine_far.at[:, o], sibv.at[:, 0, :, cols], 1)
-        for m, (missing, come) in enumerate(((first, come_up), (final, come_down))):
-            @pl.when(missing)
-            def _(m=m):
-                for j in range(3):
-                    part[1, j, m, :, cols] = jnp.zeros((rows_n, 128 if kind == "i" else WIDTH), BF)
-
-            @pl.when(jnp.logical_not(missing))
-            def _(m=m, come=come):
-                fetch(come.at[:, o], part.at[1, :, m, :, cols], 1)
-
-        def add(i, carry):
-            j = i // (rows_n // 48)
-            here = pl.ds(pl.multiple_of(lax.rem(i, rows_n // 48) * 48, 16), 48)
-            value = sibv[j, 0, here, cols].astype(F32)
-            for m in range(2):
-                value = value + part[1, j, m, here, cols].astype(F32)
-            ws[h, j, place_o, place_p, here, cols] = value.astype(BF)
-            return carry
-
-        lax.fori_loop(0, 3 * (rows_n // 48), add, 0)
-        hand_back(kind, c, "start")
-
     half = out_n // 2
 
     def grad_rows(h):
@@ -744,6 +761,14 @@
 
         lax.fori_loop(0, 2, token_tile, 0)
 
+        @pl.when(c >= 1)
+        def _():
+            pair_fetch("f", c - 1, "start")
+
+        @pl.when(c >= 2)
+        def _():
+            first_send("f", c - 2)
+
         @pl.when(c >= 2)
         def _():
             pair_send("f", c - 2, "end")
@@ -761,7 +786,7 @@
 
         @pl.when(c >= 1)
         def _():
-            pair_sum("f", c - 1)
+            pair_add("f", c - 1)
 
         pump(c + loop_pump)
 
@@ -778,10 +803,13 @@
         stage[q] = acc_n[any_span(q), :].astype(BF)
 
     scatter(staged, rs_n2, 1, d_normed_two)
-    pair_sum("f", chunks - 1)
+    first_send("f", chunks - 2)
+    pair_fetch("f", chunks - 1, "start")
+    pair_add("f", chunks - 1)
     scatter_on(staged, rs_n2, 1)
-    for time in range(1, 4):
-        line_time("f", time, chunks)
+    first_send("f", chunks - 1)
+    for k in range(steps - 1):
+        sums_of([("f", c, k) for c in range(chunks - 2)])
     scatter_wait(rs_n2, 1)
     scatter_end(staged, rs_n2, 1)
     spread(low, n2_all, 2, "end")
@@ -816,8 +844,9 @@
         act_t[:, span(q)] = act[span(q), :].T
     spill_back.wait()
     spread_on(dbr_all, 3)
-    for time in range(4, 7):
-        line_time("f", time, chunks)
+    for k in range(steps - 1):
+        sums_of([("f", c, k) for c in range(chunks - 2, chunks)])
+    sums_of([("f", c, steps - 1) for c in range(chunks - 3)])
 
     acc_n[pl.ds(seq, 8), pl.ds(0, ch)] = jnp.zeros((8, ch), F32)
     for q in range(group):
@@ -866,7 +895,10 @@
         lax.fori_loop(0, 2, intake_tile, 0)
         pair_send("i", k, "start")
         if k >= 1:
-            pair_sum("i", k - 1)
+            pair_fetch("i", k - 1, "start")
+            if k >= 2:
+                first_send("i", k - 2)
+            pair_add("i", k - 1)
 
     for n in range(4):
         col = pl.ds(n * 384, 384)
@@ -874,7 +906,11 @@
     last = chunks + blocks
     pair_o = remote(wo.at[:, 1 - b], sib_o, gs_ssem.at[last], gs_rsem.at[last], mate)
     pair_o.start()
-    pair_sum("i", blocks - 1)
+    if blocks >= 2:
+        first_send("i", blocks - 2)
+    pair_fetch("i", blocks - 1, "start")
+    pair_add("i", blocks - 1)
+    first_send("i", blocks - 1)
 
     await_bytes(sib_o, gs_rsem.at[last])
     fetch(sib_o, sibo, 1)
@@ -888,7 +924,7 @@
     def part_o(op):
         def one(k, carry):
             o2, dev = peer(k)
-            copy = remote(parto.at[o2], z_o.at[o], gz_ssem.at[last, k], up_sem.at[last, o], dev)
+            copy = remote(parto.at[o2], z_o.at[o], gz_ssem.at[last, k], come_sem.at[last, o], dev)
             if op == "start":
                 copy.start()
             else:
@@ -933,14 +969,7 @@
     lax.fori_loop(0, seg // ROW_TILE, out_rows, 0)
     fetch(low, block_out, 0)
 
-    for time in range(7, chunks + out_n - 1):
-        line_time("f", time, chunks)
-
-    def total_f(c, carry):
-        total("f", c)
-        return carry
-
-    lax.fori_loop(0, chunks, total_f, 0)
+    sums_of([("f", c, steps - 1) for c in range(chunks - 3, chunks)])
     scatter_wait(rs_n1, 3)
     scatter_end(lent, rs_n1, 3)
     fetch(rs_n1, stage.at[pl.ds(0, 3)], 0)
@@ -978,11 +1007,8 @@
     for k in range(max(0, blocks - 2), blocks):
         pair_send("i", k, "end")
 
-    def lines(time, carry):
-        line_time("i", time, blocks)
-        return carry
-
-    lax.fori_loop(1, out_n - 1, lines, 0)
+    for k in range(steps - 1):
+        sums_of([("i", c, k) for c in range(blocks)])
     plane_wait(sm_mine, ta_rsem)
     value = sm_plane[0]
     for i in range(1, 2 * group):
@@ -990,14 +1016,12 @@
     sm_sum[...] = value
     sm_z[o] = value
     far(sm_sum, sm_z.at[o], tz_ssem, tz_rsem, "start")
-    lax.fori_loop(out_n - 1, blocks + out_n - 1, lines, 0)
-    for k in range(blocks):
-        total("i", k)
+    sums_of([("i", c, steps - 1) for c in range(blocks)])
     part_o("end")
     pair_o.wait_send()
 
     def last_one(k, carry):
-        await_bytes(z_o.at[o], up_sem.at[last, peer(k)[0]])
+        await_bytes(z_o.at[o], come_sem.at[last, peer(k)[0]])
         return carry
 
     lax.fori_loop(1, out_n, last_one, 0)
@@ -1034,14 +1058,16 @@
 
     def close(c, carry):
         gather_close(c + 2)
-        line_close("f", c)
+        for k in range(steps):
+            step_send("f", c, k, "end")
         hand_back("f", c, "end")
         hand_wait("f", c)
         return carry
 
     lax.fori_loop(0, chunks, close, 0)
     for k in range(blocks):
-        line_close("i", k)
+        for step in range(steps):
+            step_send("i", k, step, "end")
         hand_back("i", k, "end")
         hand_wait("i", k)
     back_o("end")
@@ -1075,7 +1101,7 @@
         shape(group, seg, D), shape(seq, D), shape(group, seg, D), shape(group, seg, D), shape(group, seg, D),
         shape(3, seg, D), shape(3, seg, D), shape(3, seg, D), shape(3, seg, D), shape(4, 2, seg // 2, D),
         shape(chunks, 3, out_n, rows_n, WIDTH), shape(blocks, 3, out_n, rows_n, 128), shape(out_n, cblk, D),
-        *[shape(chunks, 3, out_n, rows_n, WIDTH), shape(blocks, 3, out_n, rows_n, 128)] * 3, shape(out_n, cblk, D),
+        *[shape(chunks, 3, out_n, rows_n, WIDTH), shape(blocks, 3, out_n, rows_n, 128)] * 2, shape(out_n, cblk, D),
         shape(seq, 3 * ch, dtype=F32),
     ]
     out_specs = [any_spec] * 5 + [vmem_spec] + [any_spec] * (len(outs) - 6)
@@ -1099,7 +1125,7 @@
         vm((seg // 2, D), BF),
         dma((4, 3, 2)), dma((4, group, 2)), dma((4, 2)), dma((4, 4, 2)), dma((4, 3, 2)), dma((4, 2, 2)), dma((4, 2)),
         dma((items, 2, out_n)), dma((items, out_n)), dma((items,)), dma((items,)),
-        dma((sums,)), dma((sums,)), dma((sums, out_n)), dma((sums, out_n)), dma((sums, out_n)),
+        dma((sums,)), dma((sums,)), dma((sums, out_n)), dma((sums, out_n)), dma((2,)), dma((2, out_n)),
         dma((items, group)), dma((items, group)), dma((sums, group)), dma((sums, group)), dma((1,)),
         dma((places,)), dma((places,)), dma((out_n,)), dma((out_n,)),
         dma((places,)), dma((places,)), dma((out_n,)), dma((out_n,)), dma((2,)), dma((5,)),

time: 611 us -> 512 us (0.84)
  the two profiles are of different devices: /device:TPU:1 before, /device:TPU:13 now
where the time goes in v1:
time: 512 us; the launch traced here: 502 us
  Pallas kernels  424 us (83%)
  local copies, waits for them, and re-layouts  46.6 us (9%)
  other arithmetic  29 us (6%)
    pallas_call x1, Pallas kernels, forward_backward(): pl.pallas_call(functools.partial(block_kernel, sizes), out_shape=outs, in...  424 us
    sub x6, other arithmetic, update(): weight - rate * (first_hat / (jnp.sqrt(second_hat) + ADAM_EPS) + decay *...  16.1 us

profile of v1, /device:TPU:13, one launch (start us, length us, event | category | flops | bytes accessed | tf_op | source)
XLA Modules:
  0.0 502.2 jit_solution(6546528362392276141)
XLA Ops:
  0.7 0.0 copy-start.4
  1.5 0.8 reduce-precision_dynamic-update-slice_fusion.2
  2.3 0.8 reduce-precision_dynamic-update-slice_fusion.1
  3.2 0.8 reduce-precision_dynamic-update-slice_fusion
  4.0 0.7 reduce-precision_dynamic-update-slice_fusion.3
  4.7 0.6 pad_maximum_fusion.small_own
  5.3 1.0 convert_element_type.68
  6.3 0.9 reshape.110.wo_own
  7.2 1.2 convert_element_type.67
  8.4 0.1 convert_element_type.70
  8.5 0.7 reshape.112
  9.2 1.0 reshape.107
  10.2 0.2 copy.47
  10.4 1.6 reshape.108
  11.9 2.3 copy.48
  14.3 2.1 reshape.109.wi_own
  16.4 2.2 fusion.4.bck_own
  18.6 1.2 convert_element_type.69
  19.8 3.4 reshape.111
  23.2 2.0 fusion.3
  25.2 4.0 reshape.128
  29.2 2.6 copy.62
  31.8 0.0 copy-start.17
  31.8 0.0 copy-start.18
  31.8 0.0 copy-start.8
  31.8 0.0 copy-start.14
  31.9 0.0 copy-start.15
  31.9 424.4 %shard_map.356 = (bf16[256,1536]{1,0:T(8,128)(2,1)}, bf16[256,1536]{1,0:T(8,128)(2,1)}, bf16[4,7,3,48,256]{4,3,2,1,0:T(8,128)(2,1)}, bf16[4,3,3,48,128]{4,3,2,1,...) custom-call(bf16[256,1536]{1,0:T(8,128)(2,1)} %bitcast.46, ...), custom_call_target="tpu_custom_call" | custom-call | flops 65229815808 | bytes 200000000 | tf_op jit(solution)/shard_map/pallas_call | solution.py:1133
  456.3 0.8 slice_bitcast_fusion
  457.1 0.7 slice.30
  457.8 0.0 copy-done.20
  457.8 0.6 multiply_subtract_fusion.5
  458.4 0.1 reshape.120
  458.5 0.1 reshape.121
  458.7 0.7 multiply_subtract_fusion.4
  459.3 1.1 reshape.124
  460.5 1.1 multiply_subtract_fusion.3
  461.5 0.0 copy-done.13
  461.5 0.1 convert_bitcast_fusion
  461.6 0.5 copy.52
  462.0 1.1 reshape.127
  463.2 2.9 copy.53
  466.1 3.6 reshape.123
  469.7 0.0 copy-done.5
  469.7 0.0 copy-done.9
  469.8 0.0 copy-done.10
  469.8 0.0 copy-start.7
  469.8 2.0 multiply_subtract_fusion.2
  471.7 0.3 copy-done.7
  472.1 0.9 copy.54
  473.0 3.5 reshape.118
  476.5 1.2 slice_convert_fusion.1
  477.7 0.0 copy-start.3
  477.8 0.9 copy.56
  478.7 2.2 reshape.126
  480.8 0.2 slice_convert_fusion
  481.1 1.8 copy.55
  482.9 3.8 reshape.125
  486.6 5.3 %multiply_subtract_fusion.1 = (f32[331776]{0:T(1024)}, f32[331776]{0:T(1024)}, f32[331776]{0:T(1024)}) fusion(f32[331776]{0:T(1024)} %param.33, f32[331776]{0:T(1024)} %reshape.126, f32[331776]{0:T(1024)} %param.35, f32[331776]{0:T(1024)} %param.34), kind=kLoop, calls=%fused_computation.15 | loop fusion | flops 4644864 | bytes 9289728 | tf_op jit(solution)/shard_map/sub | solution.py:34
  491.9 1.1 copy-done.6
  493.0 6.5 %multiply_subtract_fusion = (f32[663552]{0:T(1024)}, f32[663552]{0:T(1024)}, f32[663552]{0:T(1024)}) fusion(f32[663552]{0:T(1024)S(1)} %copy-done.1, f32[663552]{0:T(1024)S(1)} %copy-done.2, f32[663552]{0:T(1024)S(1)} %copy-done.6, f32[663552]{0:T(1024)} %param.31), kind=kLoop, calls=%fused_computation.6 | loop fusion | flops 9289728 | bytes 18579456 | tf_op jit(solution)/shard_map/sub | solution.py:34
  499.5 0.9 copy.71
  500.4 0.5 copy-done.11
  500.9 0.9 copy.72
  (34 shorter events, 0.1 us)
Async XLA Ops:
  0.7 7.7 %copy-start.4 = (f32[331776]{0:T(1024)S(1)}, f32[331776]{0:T(1024)}, u32[]{:S(2)}) copy-start(f32[331776]{0:T(1024)} %param.33) | copy-start | bytes 3981316
  11.9 6.7 %copy-start = (f32[663552]{0:T(1024)S(1)}, f32[663552]{0:T(1024)}, u32[]{:S(2)}) copy-start(f32[663552]{0:T(1024)} %param.30) | copy-start | bytes 7962628
  31.8 426.0 %copy-start.19 = (f32[96]{0:T(128)S(1)}, f32[96]{0:T(128)}, u32[]{:S(2)}) copy-start(f32[96]{0:T(128)} %param.36) | copy-start | bytes 1156
  31.8 426.0 %copy-start.20 = (f32[96]{0:T(128)S(1)}, f32[96]{0:T(128)}, u32[]{:S(2)}) copy-start(f32[96]{0:T(128)} %param.38) | copy-start | bytes 1156
  31.8 426.0 %copy-start.21 = (f32[96]{0:T(128)S(1)}, f32[96]{0:T(128)}, u32[]{:S(2)}) copy-start(f32[96]{0:T(128)} %param.37) | copy-start | bytes 1156
  31.8 426.8 %copy-start.16 = (f32[144]{0:T(256)S(1)}, f32[144]{0:T(256)}, u32[]{:S(2)}) copy-start(f32[144]{0:T(256)} %param.39) | copy-start | bytes 1732
  31.8 426.8 %copy-start.17 = (f32[144]{0:T(256)S(1)}, f32[144]{0:T(256)}, u32[]{:S(2)}) copy-start(f32[144]{0:T(256)} %param.41) | copy-start | bytes 1732
  31.8 426.8 %copy-start.18 = (f32[144]{0:T(256)S(1)}, f32[144]{0:T(256)}, u32[]{:S(2)}) copy-start(f32[144]{0:T(256)} %param.40) | copy-start | bytes 1732
  31.8 428.6 %copy-start.8 = (f32[73728]{0:T(1024)S(1)}, f32[73728]{0:T(1024)}, u32[]{:S(2)}) copy-start(f32[73728]{0:T(1024)} %param.27) | copy-start | bytes 884740
  31.8 428.6 %copy-start.14 = (f32[73728]{0:T(1024)S(1)}, f32[73728]{0:T(1024)}, u32[]{:S(2)}) copy-start(f32[73728]{0:T(1024)} %param.29) | copy-start | bytes 884740
  31.9 428.6 %copy-start.15 = (f32[73728]{0:T(1024)S(1)}, f32[73728]{0:T(1024)}, u32[]{:S(2)}) copy-start(f32[73728]{0:T(1024)} %param.28) | copy-start | bytes 884740
  456.3 5.2 %copy-start.13 = (bf16[4,3,3,48,128]{4,3,2,1,0:T(8,128)(2,1)S(1)}, bf16[4,3,3,48,128]{4,3,2,1,0:T(8,128)(2,1)}, u32[]{:S(2)}) copy-start(bf16[4,3,3,48,128]{4,3,2,1,0:T(8,128)(2,1)} %get-tuple-element.28) | copy-start | bytes 1327108
  466.1 3.6 copy-start.5
  466.1 3.6 copy-start.9
  466.1 3.7 copy-start.10
  469.8 2.3 copy-start.7
  477.7 3.1 copy-start.3
  486.6 5.3 %copy-start.1 = (f32[663552]{0:T(1024)S(1)}, f32[663552]{0:T(1024)}, u32[]{:S(2)}) copy-start(f32[663552]{0:T(1024)} %param.30) | copy-start | bytes 7962628
  486.6 5.3 %copy-start.2 = (f32[663552]{0:T(1024)S(1)}, f32[663552]{0:T(1024)}, u32[]{:S(2)}) copy-start(f32[663552]{0:T(1024)} %reshape.125) | copy-start | bytes 7962628
  486.6 6.4 %copy-start.6 = (f32[663552]{0:T(1024)S(1)}, f32[663552]{0:T(1024)}, u32[]{:S(2)}) copy-start(f32[663552]{0:T(1024)} %param.32) | copy-start | bytes 7962628
  493.0 6.5 %copy-start.12 = (bf16[256,1536]{1,0:T(8,128)(2,1)S(1)}, bf16[256,1536]{1,0:T(8,128)(2,1)}, u32[]{:S(2)}) copy-start(bf16[256,1536]{1,0:T(8,128)(2,1)} %get-tuple-element.26) | copy-start | bytes 2359300
  499.5 1.4 copy-start.11

commit v2 on v1

--- a/solution.py
+++ b/solution.py
@@ -738,6 +738,9 @@
 
     loop_pump = out_n + 5
 
+    def d_normed_two(q):
+        stage[q] = acc_n[any_span(q), :].astype(BF)
+
     def hidden_chunk(c, carry):
         s = lax.rem(c, 2)
         await_bytes(ws.at[s], wsem.at[s])
@@ -761,6 +764,10 @@
 
         lax.fori_loop(0, 2, token_tile, 0)
 
+        @pl.when(c == chunks - 1)
+        def _():
+            scatter(staged, rs_n2, 1, d_normed_two)
+
         @pl.when(c >= 1)
         def _():
             pair_fetch("f", c - 1, "start")
@@ -799,10 +806,6 @@
 
     lax.fori_loop(0, chunks, hidden_chunk, 0)
 
-    def d_normed_two(q):
-        stage[q] = acc_n[any_span(q), :].astype(BF)
-
-    scatter(staged, rs_n2, 1, d_normed_two)
     first_send("f", chunks - 2)
     pair_fetch("f", chunks - 1, "start")
     pair_add("f", chunks - 1)
@@ -842,8 +845,9 @@
         bck_t[pl.ds(0, ch), span(q)] = gated[span(q), :].T
         fetch(nrm_far.at[span(q)], act.at[span(q)], 0)
         act_t[:, span(q)] = act[span(q), :].T
+        if q == 1:
+            spread_on(dbr_all, 3)
     spill_back.wait()
-    spread_on(dbr_all, 3)
     for k in range(steps - 1):
         sums_of([("f", c, k) for c in range(chunks - 2, chunks)])
     sums_of([("f", c, steps - 1) for c in range(chunks - 3)])

time: 512 us -> 506 us (0.988)
  the two profiles are of different devices: /device:TPU:13 before, /device:TPU:17 now
where the time goes in v2:
time: 506 us; the launch traced here: 496 us
  Pallas kernels  419 us (83%)
  local copies, waits for them, and re-layouts  46.6 us (9%)
  other arithmetic  29 us (6%)
    pallas_call x1, Pallas kernels, forward_backward(): pl.pallas_call(functools.partial(block_kernel, sizes), out_shape=outs, in...  419 us
    sub x6, other arithmetic, update(): weight - rate * (first_hat / (jnp.sqrt(second_hat) + ADAM_EPS) + decay *...  16.1 us

profile of v2, /device:TPU:17, one launch (start us, length us, event | category | flops | bytes accessed | tf_op | source)
XLA Modules:
  0.0 496.4 jit_solution(12731723261486149744)
XLA Ops:
  0.7 0.0 copy-start.4
  1.5 0.8 reduce-precision_dynamic-update-slice_fusion.2
  2.3 0.8 reduce-precision_dynamic-update-slice_fusion.1
  3.2 0.8 reduce-precision_dynamic-update-slice_fusion
  4.0 0.7 reduce-precision_dynamic-update-slice_fusion.3
  4.7 0.6 pad_maximum_fusion.small_own
  5.3 1.0 convert_element_type.68
  6.3 0.9 reshape.110.wo_own
  7.2 1.2 convert_element_type.67
  8.4 0.0 copy-done.4
  8.4 0.1 convert_element_type.70
  8.5 0.7 reshape.112
  9.2 1.0 reshape.107
  10.2 0.2 copy.47
  10.4 1.6 reshape.108
  11.9 2.3 copy.48
  14.3 2.1 reshape.109.wi_own
  16.4 2.2 fusion.4.bck_own
  18.6 0.0 copy-done
  18.6 1.2 convert_element_type.69
  19.8 3.4 reshape.111
  23.2 2.0 fusion.3
  25.2 4.0 reshape.128
  29.2 2.6 copy.62
  31.8 0.0 copy-start.17
  31.8 0.0 copy-start.18
  31.8 0.0 copy-start.8
  31.8 0.0 copy-start.14
  31.9 0.0 copy-start.15
  31.9 418.6 %shard_map.356 = (bf16[256,1536]{1,0:T(8,128)(2,1)}, bf16[256,1536]{1,0:T(8,128)(2,1)}, bf16[4,7,3,48,256]{4,3,2,1,0:T(8,128)(2,1)}, bf16[4,3,3,48,128]{4,3,2,1,...) custom-call(bf16[256,1536]{1,0:T(8,128)(2,1)} %bitcast.46, ...), custom_call_target="tpu_custom_call" | custom-call | flops 65229815808 | bytes 200000000 | tf_op jit(solution)/shard_map/pallas_call | solution.py:1137
  450.4 0.8 slice_bitcast_fusion
  451.2 0.7 slice.30
  451.9 0.6 multiply_subtract_fusion.5
  452.6 0.1 reshape.120
  452.7 0.1 reshape.121
  452.8 0.7 multiply_subtract_fusion.4
  453.5 1.1 reshape.124
  454.6 0.0 copy-done.8
  454.6 0.0 copy-done.14
  454.6 0.0 copy-done.15
  454.6 1.1 multiply_subtract_fusion.3
  455.6 0.1 convert_bitcast_fusion
  455.7 0.5 copy.52
  456.2 1.1 reshape.127
  457.3 2.9 copy.53
  460.2 3.6 reshape.123
  463.9 2.0 multiply_subtract_fusion.2
  465.9 0.3 copy-done.7
  466.2 0.9 copy.54
  467.1 3.5 reshape.118
  470.7 1.2 slice_convert_fusion.1
  471.9 0.0 copy-start.3
  471.9 0.9 copy.56
  472.8 2.2 reshape.126
  475.0 0.2 slice_convert_fusion
  475.2 1.8 copy.55
  477.0 3.8 reshape.125
  480.8 5.3 %multiply_subtract_fusion.1 = (f32[331776]{0:T(1024)}, f32[331776]{0:T(1024)}, f32[331776]{0:T(1024)}) fusion(f32[331776]{0:T(1024)} %param.33, f32[331776]{0:T(1024)} %reshape.126, f32[331776]{0:T(1024)} %param.35, f32[331776]{0:T(1024)} %param.34), kind=kLoop, calls=%fused_computation.15 | loop fusion | flops 4644864 | bytes 9289728 | tf_op jit(solution)/shard_map/sub | solution.py:34
  486.1 0.0 copy-done.1
  486.1 1.1 copy-done.6
  487.1 6.5 %multiply_subtract_fusion = (f32[663552]{0:T(1024)}, f32[663552]{0:T(1024)}, f32[663552]{0:T(1024)}) fusion(f32[663552]{0:T(1024)S(1)} %copy-done.1, f32[663552]{0:T(1024)S(1)} %copy-done.2, f32[663552]{0:T(1024)S(1)} %copy-done.6, f32[663552]{0:T(1024)} %param.31), kind=kLoop, calls=%fused_computation.6 | loop fusion | flops 9289728 | bytes 18579456 | tf_op jit(solution)/shard_map/sub | solution.py:34
  493.6 0.9 copy.71
  494.5 0.5 copy-done.11
  495.0 0.9 copy.72
  (34 shorter events, 0.1 us)
Async XLA Ops:
  0.7 7.7 %copy-start.4 = (f32[331776]{0:T(1024)S(1)}, f32[331776]{0:T(1024)}, u32[]{:S(2)}) copy-start(f32[331776]{0:T(1024)} %param.33) | copy-start | bytes 3981316
  11.9 6.7 %copy-start = (f32[663552]{0:T(1024)S(1)}, f32[663552]{0:T(1024)}, u32[]{:S(2)}) copy-start(f32[663552]{0:T(1024)} %param.30) | copy-start | bytes 7962628
  31.8 420.1 %copy-start.19 = (f32[96]{0:T(128)S(1)}, f32[96]{0:T(128)}, u32[]{:S(2)}) copy-start(f32[96]{0:T(128)} %param.36) | copy-start | bytes 1156
  31.8 420.1 %copy-start.20 = (f32[96]{0:T(128)S(1)}, f32[96]{0:T(128)}, u32[]{:S(2)}) copy-start(f32[96]{0:T(128)} %param.38) | copy-start | bytes 1156
  31.8 420.1 %copy-start.21 = (f32[96]{0:T(128)S(1)}, f32[96]{0:T(128)}, u32[]{:S(2)}) copy-start(f32[96]{0:T(128)} %param.37) | copy-start | bytes 1156
  31.8 421.0 %copy-start.16 = (f32[144]{0:T(256)S(1)}, f32[144]{0:T(256)}, u32[]{:S(2)}) copy-start(f32[144]{0:T(256)} %param.39) | copy-start | bytes 1732
  31.8 421.0 %copy-start.17 = (f32[144]{0:T(256)S(1)}, f32[144]{0:T(256)}, u32[]{:S(2)}) copy-start(f32[144]{0:T(256)} %param.41) | copy-start | bytes 1732
  31.8 421.0 %copy-start.18 = (f32[144]{0:T(256)S(1)}, f32[144]{0:T(256)}, u32[]{:S(2)}) copy-start(f32[144]{0:T(256)} %param.40) | copy-start | bytes 1732
  31.8 422.7 %copy-start.8 = (f32[73728]{0:T(1024)S(1)}, f32[73728]{0:T(1024)}, u32[]{:S(2)}) copy-start(f32[73728]{0:T(1024)} %param.27) | copy-start | bytes 884740
  31.8 422.7 %copy-start.14 = (f32[73728]{0:T(1024)S(1)}, f32[73728]{0:T(1024)}, u32[]{:S(2)}) copy-start(f32[73728]{0:T(1024)} %param.29) | copy-start | bytes 884740
  31.9 422.7 %copy-start.15 = (f32[73728]{0:T(1024)S(1)}, f32[73728]{0:T(1024)}, u32[]{:S(2)}) copy-start(f32[73728]{0:T(1024)} %param.28) | copy-start | bytes 884740
  450.4 5.2 %copy-start.13 = (bf16[4,3,3,48,128]{4,3,2,1,0:T(8,128)(2,1)S(1)}, bf16[4,3,3,48,128]{4,3,2,1,0:T(8,128)(2,1)}, u32[]{:S(2)}) copy-start(bf16[4,3,3,48,128]{4,3,2,1,0:T(8,128)(2,1)} %get-tuple-element.28) | copy-start | bytes 1327108
  460.2 3.6 copy-start.5
  460.2 3.6 copy-start.9
  460.2 3.7 copy-start.10
  463.9 2.3 copy-start.7
  471.9 3.1 copy-start.3
  480.8 5.3 %copy-start.1 = (f32[663552]{0:T(1024)S(1)}, f32[663552]{0:T(1024)}, u32[]{:S(2)}) copy-start(f32[663552]{0:T(1024)} %param.30) | copy-start | bytes 7962628
  480.8 5.3 %copy-start.2 = (f32[663552]{0:T(1024)S(1)}, f32[663552]{0:T(1024)}, u32[]{:S(2)}) copy-start(f32[663552]{0:T(1024)} %reshape.125) | copy-start | bytes 7962628
  480.8 6.4 %copy-start.6 = (f32[663552]{0:T(1024)S(1)}, f32[663552]{0:T(1024)}, u32[]{:S(2)}) copy-start(f32[663552]{0:T(1024)} %param.32) | copy-start | bytes 7962628
  487.1 6.5 %copy-start.12 = (bf16[256,1536]{1,0:T(8,128)(2,1)S(1)}, bf16[256,1536]{1,0:T(8,128)(2,1)}, u32[]{:S(2)}) copy-start(bf16[256,1536]{1,0:T(8,128)(2,1)} %get-tuple-element.26) | copy-start | bytes 2359300
  493.6 1.4 copy-start.11
